TPU v7x, 32 devices: a whole 2x2x4 slice. The times are simulated.
32 devices in a mesh: dp: 4 (over y, x), seq: 4 (over z), tensor: 2 (over core).
Axes of the slice: x: 2, y: 2, z: 4, core: 2. Of those that a mesh axis runs over, the one named last changes fastest.
Arguments:
- clips: bfloat16 [16, 8, 192, 768], P('dp', 'seq'), may hold values from -6 to 6
- cotangent: bfloat16 [16, 8, 192, 768], P('dp', 'seq'), may hold values from -6 to 6
- clip_counts: int32 [4], P('dp'), may hold values from 1 to 4, as said below
- norm_params: float32 [6, 768], replicated, may hold values from -0.6 to 1.5
- norm_moment: float32 [6, 768], replicated, may hold values from 737.28 to 14745.6
- qkv_weight: float32 [2, 3, 768, 768], P(None, None, ('dp', 'seq'), 'tensor'), may hold values from -0.21875 to 0.21875
- qkv_row: float32 [2, 3, 768], P(None, None, ('dp', 'seq')), may hold values from 737.28 to 14745.6
- qkv_col: float32 [2, 3, 768], P(None, None, 'tensor'), may hold values from 737.28 to 14745.6
- out_weight: float32 [2, 768, 768], P(None, ('dp', 'seq'), 'tensor'), may hold values from -0.875 to 0.875
- out_row: float32 [2, 768], P(None, ('dp', 'seq')), may hold values from 737.28 to 14745.6
- out_col: float32 [2, 768], P(None, 'tensor'), may hold values from 737.28 to 14745.6
- ffn_weight: float32 [2, 768, 3072], P(None, ('dp', 'seq'), 'tensor'), may hold values from -0.21875 to 0.21875
- ffn_row: float32 [2, 768], P(None, ('dp', 'seq')), may hold values from 737.28 to 14745.6
- ffn_col: float32 [2, 3072], P(None, 'tensor'), may hold values from 737.28 to 14745.6
Outputs:
- layer_out: bfloat16 [16, 8, 192, 768], P('dp', 'seq')
- grad_input: float32 [16, 8, 192, 768], P('dp', 'seq')
- norm_grad: float32 [6, 768], replicated
- norm_moment_new: float32 [6, 768], replicated
- norm_new: float32 [6, 768], replicated
- qkv_grad: float32 [2, 3, 768, 768], P(None, None, ('dp', 'seq'), 'tensor')
- qkv_new: float32 [2, 3, 768, 768], P(None, None, ('dp', 'seq'), 'tensor')
- qkv_row_new: float32 [2, 3, 768], P(None, None, ('dp', 'seq'))
- qkv_col_new: float32 [2, 3, 768], P(None, None, 'tensor')
- out_grad: float32 [2, 768, 768], P(None, ('dp', 'seq'), 'tensor')
- out_new: float32 [2, 768, 768], P(None, ('dp', 'seq'), 'tensor')
- out_row_new: float32 [2, 768], P(None, ('dp', 'seq'))
- out_col_new: float32 [2, 768], P(None, 'tensor')
- ffn_grad: float32 [2, 768, 3072], P(None, ('dp', 'seq'), 'tensor')
- ffn_new: float32 [2, 768, 3072], P(None, ('dp', 'seq'), 'tensor')
- ffn_row_new: float32 [2, 768], P(None, ('dp', 'seq'))
- ffn_col_new: float32 [2, 3072], P(None, 'tensor')
Inputs may be any that keep to these rules, and one draw needn't show every extreme that they name: `clip_counts`: in every draw some data group is full (4 clips) and another holds one clip.
All inputs are finite; a program needn't handle non-finite values.
Results may differ from a plain program's by a relative error of at most 0.017.
The roundings to bfloat16 on the way count: a program that leaves them out, or rounds other values in their place, can miss the bound.
Values may be sent and summed in bfloat16 or wider, within the bound.
A program may use at most 256 MiB of HBM per device.

v0:
```python
import jax
import jax.numpy as jnp
from jax import lax
from jax.sharding import PartitionSpec as P

HEAD_DIM = 64
MICRO = 2
STEP = 8


EPS = 1e-06
EPS_ONE = 1e-30
SCALE = 0.125
RATE_QKV = 0.02
RATE_OUT = 0.07
RATE_NORM = 0.25
TEMPORAL = ("cfphd", "cgphd", "cphfg")
SPATIAL = ("cfphd", "cfkhd", "cfhpk")


def layer_norm(values, gain_vec, bias_vec):
    centred = values - jnp.mean(values, -1, keepdims=True)
    variance = jnp.mean(centred * centred, -1, keepdims=True)
    return centred * lax.rsqrt(variance + EPS) * gain_vec + bias_vec


def norm_back(values, gain_vec, bias_vec, upstream):
    unused, pullback = jax.vjp(layer_norm, values, gain_vec, bias_vec)
    return pullback(upstream)


def gelu_exact(values):
    return jax.nn.gelu(values, approximate=False)


def form_pair(first, second, target):
    return first + "," + second + "->" + target


def split_heads(piece):
    return piece.reshape(piece.shape[:-1] + (piece.shape[-1] // HEAD_DIM, HEAD_DIM))


def join_heads(values):
    return values.reshape(values.shape[:-2] + (values.shape[-2] * values.shape[-1],))


def to_places(stacked):
    return lax.all_to_all(stacked, "seq", split_axis=3, concat_axis=2, tiled=True)


def to_frames(stacked):
    return lax.all_to_all(stacked, "seq", split_axis=2, concat_axis=3, tiled=True)


def tensor_total(partial_term):
    return lax.psum(partial_term, "tensor")


def attend(stacked, form_set):
    q_form, k_form, s_form = form_set
    query_part = split_heads(stacked[0])
    key_part = split_heads(stacked[1])
    value_part = split_heads(stacked[2])
    scores = (
        jnp.einsum(
            form_pair(q_form, k_form, s_form),
            query_part,
            key_part,
            preferred_element_type=jnp.float32,
        )
        * SCALE
    )
    row_top = jnp.max(scores, -1, keepdims=True)
    exp_scores = jnp.exp(scores - row_top)
    denom_sum = jnp.sum(exp_scores, -1, keepdims=True)
    soft_weights = (exp_scores / denom_sum).astype(jnp.bfloat16)
    mixed = jnp.einsum(
        form_pair(s_form, k_form, q_form),
        soft_weights,
        value_part,
        preferred_element_type=jnp.float32,
    )
    return (join_heads(mixed).astype(jnp.bfloat16), row_top + jnp.log(denom_sum))


def attend_back(stacked, log_total, grad_mixed, form_set):
    q_form, k_form, s_form = form_set
    query_part = split_heads(stacked[0])
    key_part = split_heads(stacked[1])
    value_part = split_heads(stacked[2])
    grad_heads = split_heads(grad_mixed)
    scores = (
        jnp.einsum(
            form_pair(q_form, k_form, s_form),
            query_part,
            key_part,
            preferred_element_type=jnp.float32,
        )
        * SCALE
    )
    soft_full = jnp.exp(scores - log_total)
    grad_soft = jnp.einsum(
        form_pair(q_form, k_form, s_form),
        grad_heads,
        value_part,
        preferred_element_type=jnp.float32,
    )
    centre = jnp.sum(soft_full * grad_soft, -1, keepdims=True)
    grad_scores = (soft_full * (grad_soft - centre)).astype(jnp.bfloat16)
    grad_query = (
        jnp.einsum(
            form_pair(s_form, k_form, q_form),
            grad_scores,
            key_part,
            preferred_element_type=jnp.float32,
        )
        * SCALE
    ).astype(jnp.bfloat16)
    grad_key = (
        jnp.einsum(
            form_pair(s_form, q_form, k_form),
            grad_scores,
            query_part,
            preferred_element_type=jnp.float32,
        )
        * SCALE
    ).astype(jnp.bfloat16)
    grad_value = jnp.einsum(
        form_pair(s_form, q_form, k_form),
        soft_full.astype(jnp.bfloat16),
        grad_heads,
        preferred_element_type=jnp.float32,
    ).astype(jnp.bfloat16)
    return jnp.stack([join_heads(grad_query), join_heads(grad_key), join_heads(grad_value)])


def micro_step(inputs_low, upstream_low, alive_part, gathered, norm_params):
    proj_w, out_w, ffn_w = gathered
    inputs = inputs_low.astype(jnp.float32)
    normed_one = layer_norm(inputs, norm_params[0], norm_params[3]).astype(jnp.bfloat16)
    qkv_one = jnp.einsum(
        "cfpd,sde->scfpe", normed_one, proj_w[0], preferred_element_type=jnp.float32
    ).astype(jnp.bfloat16)
    places = to_places(qkv_one)
    mixed_places, log_one = attend(places, TEMPORAL)
    mixed_one = to_frames(mixed_places[None])[0]
    first = inputs + tensor_total(
        jnp.einsum("cfpe,de->cfpd", mixed_one, out_w[0], preferred_element_type=jnp.float32)
    )
    normed_two = layer_norm(first, norm_params[1], norm_params[4]).astype(jnp.bfloat16)
    qkv_two = jnp.einsum(
        "cfpd,sde->scfpe", normed_two, proj_w[1], preferred_element_type=jnp.float32
    ).astype(jnp.bfloat16)
    mixed_two, log_two = attend(qkv_two, SPATIAL)
    second = first + tensor_total(
        jnp.einsum("cfpe,de->cfpd", mixed_two, out_w[1], preferred_element_type=jnp.float32)
    )
    normed_three = layer_norm(second, norm_params[2], norm_params[5]).astype(jnp.bfloat16)
    hidden = jnp.einsum("cfpd,dm->cfpm", normed_three, ffn_w[0], preferred_element_type=jnp.float32)
    active_full, gelu_pull = jax.vjp(gelu_exact, hidden)
    active = active_full.astype(jnp.bfloat16)
    result = second + tensor_total(
        jnp.einsum("cfpm,dm->cfpd", active, ffn_w[1], preferred_element_type=jnp.float32)
    )
    upstream = upstream_low.astype(jnp.float32) * alive_part[:, None, None, None]
    grad_low = upstream.astype(jnp.bfloat16)
    grad_ffn_out = jnp.einsum("cfpd,cfpm->dm", grad_low, active, preferred_element_type=jnp.float32)
    grad_active = jnp.einsum(
        "cfpd,dm->cfpm", grad_low, ffn_w[1], preferred_element_type=jnp.float32
    )
    grad_hidden = gelu_pull(grad_active)[0].astype(jnp.bfloat16)
    grad_ffn_in = jnp.einsum(
        "cfpd,cfpm->dm", normed_three, grad_hidden, preferred_element_type=jnp.float32
    )
    grad_normed = tensor_total(
        jnp.einsum("cfpm,dm->cfpd", grad_hidden, ffn_w[0], preferred_element_type=jnp.float32)
    )
    back_three, gain_three, bias_three = norm_back(
        second, norm_params[2], norm_params[5], grad_normed
    )
    upstream = upstream + back_three
    grad_low = upstream.astype(jnp.bfloat16)
    grad_out_two = jnp.einsum(
        "cfpd,cfpe->de", grad_low, mixed_two, preferred_element_type=jnp.float32
    )
    grad_mixed_two = jnp.einsum(
        "cfpd,de->cfpe", grad_low, out_w[1], preferred_element_type=jnp.float32
    ).astype(jnp.bfloat16)
    grad_qkv_two = attend_back(qkv_two, log_two, grad_mixed_two, SPATIAL)
    grad_proj_two = jnp.einsum(
        "cfpd,scfpe->sde", normed_two, grad_qkv_two, preferred_element_type=jnp.float32
    )
    grad_normed = tensor_total(
        jnp.einsum("scfpe,sde->cfpd", grad_qkv_two, proj_w[1], preferred_element_type=jnp.float32)
    )
    back_two, gain_two, bias_two = norm_back(first, norm_params[1], norm_params[4], grad_normed)
    upstream = upstream + back_two
    grad_low = upstream.astype(jnp.bfloat16)
    grad_out_one = jnp.einsum(
        "cfpd,cfpe->de", grad_low, mixed_one, preferred_element_type=jnp.float32
    )
    grad_mixed_one = jnp.einsum(
        "cfpd,de->cfpe", grad_low, out_w[0], preferred_element_type=jnp.float32
    ).astype(jnp.bfloat16)
    grad_places = attend_back(places, log_one, to_places(grad_mixed_one[None])[0], TEMPORAL)
    grad_qkv_one = to_frames(grad_places)
    grad_proj_one = jnp.einsum(
        "cfpd,scfpe->sde", normed_one, grad_qkv_one, preferred_element_type=jnp.float32
    )
    grad_normed = tensor_total(
        jnp.einsum("scfpe,sde->cfpd", grad_qkv_one, proj_w[0], preferred_element_type=jnp.float32)
    )
    back_one, gain_one, bias_one = norm_back(inputs, norm_params[0], norm_params[3], grad_normed)
    upstream = upstream + back_one
    weight_grads = (
        jnp.stack([grad_proj_one, grad_proj_two]),
        jnp.stack([grad_out_one, grad_out_two]),
        jnp.stack([grad_ffn_in, grad_ffn_out]),
    )
    norm_grads = jnp.stack([gain_one, gain_two, gain_three, bias_one, bias_two, bias_three])
    return (result.astype(jnp.bfloat16), upstream, weight_grads, norm_grads)


def per_device(
    clips,
    cotangent,
    clip_counts,
    norm_params,
    norm_moment,
    qkv_weight,
    qkv_row,
    qkv_col,
    out_weight,
    out_row,
    out_col,
    ffn_weight,
    ffn_row,
    ffn_col,
):
    slot_count = clips.shape[0]
    per_batch = slot_count // MICRO
    model_width = clips.shape[3]
    decay_rate = 1.0 - STEP ** (-0.8)
    live_count = clip_counts[0]
    alive_mask = (jnp.arange(slot_count, dtype=jnp.int32) < live_count).astype(jnp.float32)
    shards = (
        qkv_weight.astype(jnp.bfloat16),
        out_weight.astype(jnp.bfloat16),
        ffn_weight.astype(jnp.bfloat16),
    )
    reduced = (jnp.zeros_like(qkv_weight), jnp.zeros_like(out_weight), jnp.zeros_like(ffn_weight))
    norm_sum = jnp.zeros_like(norm_params)
    results = []
    input_grads = []
    for micro_index in range(MICRO):
        lower = micro_index * per_batch
        gathered = (
            lax.all_gather(shards[0], ("dp", "seq"), axis=2, tiled=True),
            lax.all_gather(shards[1], ("dp", "seq"), axis=1, tiled=True),
            lax.all_gather(shards[2], ("dp", "seq"), axis=1, tiled=True),
        )
        result, grad_in, weight_grads, norm_grads = micro_step(
            clips[lower : lower + per_batch],
            cotangent[lower : lower + per_batch],
            alive_mask[lower : lower + per_batch],
            gathered,
            norm_params,
        )
        results.append(result)
        input_grads.append(grad_in)
        norm_sum = norm_sum + norm_grads
        pieces = (
            lax.psum_scatter(weight_grads[0], ("dp", "seq"), scatter_dimension=2, tiled=True),
            lax.psum_scatter(weight_grads[1], ("dp", "seq"), scatter_dimension=1, tiled=True),
            lax.psum_scatter(weight_grads[2], ("dp", "seq"), scatter_dimension=1, tiled=True),
        )
        reduced = jax.tree.map(jnp.add, reduced, pieces)
    weights_old = (qkv_weight, out_weight, ffn_weight)
    row_states = (qkv_row, out_row, ffn_row)
    col_states = (qkv_col, out_col, ffn_col)
    squares = [grad_mat * grad_mat + EPS_ONE for grad_mat in reduced]
    row_part = [jnp.sum(square_mat, -1) for square_mat in squares]
    total_part = [jnp.sum(square_mat, (-2, -1)) for square_mat in squares]
    section_one = lax.psum(
        (row_part[0], row_part[1], row_part[2], total_part[0], total_part[1], total_part[2]),
        "tensor",
    )
    col_part = [jnp.sum(square_mat, -2) for square_mat in squares]
    old_part = [jnp.sum(row_state, -1) for row_state in row_states]
    section_two = lax.psum(
        (
            col_part[0],
            col_part[1],
            col_part[2],
            section_one[3],
            section_one[4],
            section_one[5],
            old_part[0],
            old_part[1],
            old_part[2],
            norm_sum,
        ),
        ("dp", "seq"),
    )
    norm_grad = section_two[9]
    tensor_ways = lax.axis_size("tensor")
    rates = (
        jnp.float32(RATE_QKV),
        jnp.float32(RATE_OUT),
        jnp.array([0.02, 0.01], jnp.float32).reshape(2, 1, 1),
    )
    new_weights = []
    row_news = []
    col_news = []
    for which in range(3):
        columns_all = reduced[which].shape[-1] * tensor_ways
        row_new = (
            decay_rate * row_states[which] + (1.0 - decay_rate) * section_one[which] / columns_all
        )
        col_new = (
            decay_rate * col_states[which] + (1.0 - decay_rate) * section_two[which] / model_width
        )
        row_mean = decay_rate * section_two[6 + which] / model_width + (
            1.0 - decay_rate
        ) * section_two[3 + which] / (model_width * columns_all)
        second = row_new[..., :, None] * col_new[..., None, :] / row_mean[..., None, None]
        update = reduced[which] * lax.rsqrt(second)
        new_weights.append(weights_old[which] - rates[which] * update)
        row_news.append(row_new)
        col_news.append(col_new)
    norm_moment_new = decay_rate * norm_moment + (1.0 - decay_rate) * (
        norm_grad * norm_grad + EPS_ONE
    )
    norm_update = norm_grad * lax.rsqrt(norm_moment_new)
    norm_rms = jnp.sqrt(jnp.mean(norm_update * norm_update, -1, keepdims=True))
    norm_new = norm_params - RATE_NORM * norm_update / jnp.maximum(1.0, norm_rms)
    layer_out = jnp.concatenate(results, 0)
    grad_input = jnp.concatenate(input_grads, 0)
    return (
        layer_out,
        grad_input,
        norm_grad,
        norm_moment_new,
        norm_new,
        reduced[0],
        new_weights[0],
        row_news[0],
        col_news[0],
        reduced[1],
        new_weights[1],
        row_news[1],
        col_news[1],
        reduced[2],
        new_weights[2],
        row_news[2],
        col_news[2],
    )


def solution(mesh):
    in_specs = (
        P("dp", "seq", None, None),
        P("dp", "seq", None, None),
        P("dp"),
        P(),
        P(),
        P(None, None, ("dp", "seq"), "tensor"),
        P(None, None, ("dp", "seq")),
        P(None, None, "tensor"),
        P(None, ("dp", "seq"), "tensor"),
        P(None, ("dp", "seq")),
        P(None, "tensor"),
        P(None, ("dp", "seq"), "tensor"),
        P(None, ("dp", "seq")),
        P(None, "tensor"),
    )
    out_specs = (
        P("dp", "seq", None, None),
        P("dp", "seq", None, None),
        P(),
        P(),
        P(),
        P(None, None, ("dp", "seq"), "tensor"),
        P(None, None, ("dp", "seq"), "tensor"),
        P(None, None, ("dp", "seq")),
        P(None, None, "tensor"),
        P(None, ("dp", "seq"), "tensor"),
        P(None, ("dp", "seq"), "tensor"),
        P(None, ("dp", "seq")),
        P(None, "tensor"),
        P(None, ("dp", "seq"), "tensor"),
        P(None, ("dp", "seq"), "tensor"),
        P(None, ("dp", "seq")),
        P(None, "tensor"),
    )
    return jax.shard_map(
        per_device, mesh=mesh, in_specs=in_specs, out_specs=out_specs, check_vma=False
    )
```

profile of v0, /device:TPU:0, one launch (start us, length us, event | category | flops | bytes accessed | tf_op | source)
XLA Modules:
  0.0 1348.4 jit_solution(2167058359178315986)
XLA Ops:
  13.7 71.7 %all-gather.4.cloned.1.call-done = bf16[2,3,768,384]{3,2,1,0:T(8,128)(2,1)} async-done(((bf16[2,3,48,384]{3,2,1,0:T(8,128)(2,1)}), bf16[2,3,768,384]{3,2,1,0:T(8,128)(2,1)}) %all-gather.4.cloned.1.call-update) | async-done | bytes 3538960 | tf_op jit(solution)/shard_map/all_gather | solution.py:259
  102.7 33.8 %all-to-all-done.2 = bf16[3,2,2,192,384]{4,2,1,0,3:T(2,128)(2,1)} async-done(((bf16[3,2,2,192,384]{4,2,1,0,3:T(2,128)(2,1)}), bf16[3,2,2,192,384]{4,2,1,0,3:T(2,128)(2,1)}, u32[]{:S(2)}, u32[]{:S(2)}) %all-to-all-start.2) | async-done | bytes 1769504 | tf_op jit(solution)/shard_map/all_to_all | solution.py:49
  163.4 19.9 %all-to-all-done = bf16[3,2,2,192,384]{4,2,1,0,3:T(2,128)(2,1)} async-done(((bf16[3,2,2,192,384]{4,2,1,0,3:T(2,128)(2,1)}), bf16[3,2,2,192,384]{4,2,1,0,3:T(2,128)(2,1)}, u32[]{:S(2)}, u32[]{:S(2)}) %all-to-all-start) | async-done | bytes 1769504 | tf_op jit(solution)/shard_map/all_to_all | solution.py:49
  221.1 13.8 %all-to-all-done.1 = bf16[1,2,8,48,384]{4,3,1,0,2:T(8,128)(2,1)} async-done(((bf16[1,2,8,48,384]{4,3,1,0,2:T(8,128)(2,1)}), bf16[1,2,8,48,384]{4,3,1,0,2:T(8,128)(2,1)}, u32[]{:S(2)}, u32[]{:S(2)}) %all-to-all-start.1) | async-done | bytes 589856 | tf_op jit(solution)/shard_map/all_to_all | solution.py:53
  243.0 27.3 %all-reduce.25.cloned.1.call-done = (f32[2,2,192,768]{3,2,1,0:T(8,128)}, f32[2,2,192,768]{3,2,1,0:T(8,128)}) async-done(((f32[2,2,192,768]{3,2,1,0:T(8,128)}, f32[2,2,192,768]{3,2,1,0:T(8,128)}), (f32[2,2,192,768]{3,2,1,0:T(8,128)}, f32[2,2,192,768]{3,2,1,0:T(8,128)})) %all-reduce.25.cloned.1.call-update) | async-done | bytes 4718608 | tf_op jit(solution)/shard_map/psum | solution.py:57
  312.9 27.2 %all-reduce.23.cloned.1.call-done = (f32[2,2,192,768]{3,2,1,0:T(8,128)}, f32[2,2,192,768]{3,2,1,0:T(8,128)}) async-done(((f32[2,2,192,768]{3,2,1,0:T(8,128)}, f32[2,2,192,768]{3,2,1,0:T(8,128)}), (f32[2,2,192,768]{3,2,1,0:T(8,128)}, f32[2,2,192,768]{3,2,1,0:T(8,128)})) %all-reduce.23.cloned.1.call-update) | async-done | bytes 4718608 | tf_op jit(solution)/shard_map/psum | solution.py:57
  348.3 76.2 %all-gather.8.cloned.1.call-done = bf16[2,768,1536]{2,1,0:T(8,128)(2,1)} async-done(((bf16[2,48,1536]{2,1,0:T(8,128)(2,1)}), bf16[2,768,1536]{2,1,0:T(8,128)(2,1)}) %all-gather.8.cloned.1.call-update) | async-done | bytes 4718608 | tf_op jit(solution)/shard_map/all_gather | solution.py:261
  424.6 5.7 fusion.87
  430.3 11.5 multiply_convert_fusion.2
  445.1 11.5 multiply_convert_fusion.3
  474.5 25.1 %all-reduce.21.cloned.1.call-done = (f32[2,2,192,768]{3,2,1,0:T(8,128)}, f32[2,2,192,768]{3,2,1,0:T(8,128)}) async-done(((f32[2,2,192,768]{3,2,1,0:T(8,128)}, f32[2,2,192,768]{3,2,1,0:T(8,128)}), (f32[2,2,192,768]{3,2,1,0:T(8,128)}, f32[2,2,192,768]{3,2,1,0:T(8,128)})) %all-reduce.21.cloned.1.call-update) | async-done | bytes 4718608 | tf_op jit(solution)/shard_map/psum | solution.py:57
  499.7 5.7 multiply_reduce_fusion.4
  573.3 24.7 %all-reduce.19.cloned.1.call-done = (f32[2,2,192,768]{3,2,1,0:T(8,128)}, f32[2,2,192,768]{3,2,1,0:T(8,128)}) async-done(((f32[2,2,192,768]{3,2,1,0:T(8,128)}, f32[2,2,192,768]{3,2,1,0:T(8,128)}), (f32[2,2,192,768]{3,2,1,0:T(8,128)}, f32[2,2,192,768]{3,2,1,0:T(8,128)})) %all-reduce.19.cloned.1.call-update) | async-done | bytes 4718608 | tf_op jit(solution)/shard_map/psum | solution.py:57
  646.0 14.2 %all-to-all-done.4 = bf16[1,2,2,192,384]{4,2,1,0,3:T(2,128)(2,1)} async-done(((bf16[1,2,2,192,384]{4,2,1,0,3:T(2,128)(2,1)}), bf16[1,2,2,192,384]{4,2,1,0,3:T(2,128)(2,1)}, u32[]{:S(2)}, u32[]{:S(2)}) %all-to-all-start.4) | async-done | bytes 589856 | tf_op jit(solution)/shard_map/all_to_all | solution.py:49
  696.6 5.4 all-to-all-start.5
  735.6 13.3 all-to-all-done.5
  753.8 5.9 convolution_bitcast_fusion.6
  766.3 30.8 %all-to-all-done.7 = bf16[3,2,8,48,384]{4,3,1,0,2:T(8,128)(2,1)} async-done(((bf16[3,2,8,48,384]{4,3,1,0,2:T(8,128)(2,1)}), bf16[3,2,8,48,384]{4,3,1,0,2:T(8,128)(2,1)}, u32[]{:S(2)}, u32[]{:S(2)}) %all-to-all-start.7) | async-done | bytes 1769504 | tf_op jit(solution)/shard_map/all_to_all | solution.py:53
  809.2 13.7 %copy.482 = f32[2,3,768,384]{3,0,1,2:T(2,128)} copy(f32[2,3,768,384]{2,3,1,0:T(8,128)} %maximum_add_fusion.1) | data formatting | bytes 14155776 | tf_op jit(solution)/shard_map/add | solution.py:278
  823.2 6.0 fusion.114
  844.0 121.4 %reduce-scatter.5.cloned.1.call-done = f32[2,48,1536]{2,1,0:T(8,128)} async-done(((f32[2,768,1536]{2,1,0:T(8,128)}), f32[2,48,1536]{2,1,0:T(8,128)}) %reduce-scatter.5.cloned.1.call-update) | async-done | bytes 589840 | tf_op jit(solution)/shard_map/reduce_scatter | solution.py:276
  966.8 230.3 %all-reduce.15.cloned.1.call-done = f32[2,3,768,384]{3,0,1,2:T(2,128)} async-done(((f32[2,3,768,384]{3,0,1,2:T(2,128)}), f32[2,3,768,384]{3,0,1,2:T(2,128)}) %all-reduce.15.cloned.1.call-update) | async-done | bytes 7077904
  1202.5 38.0 %all-reduce.17.cloned.1.call-done = (f32[2,2,192,768]{3,2,1,0:T(8,128)}, f32[2,2,192,768]{3,2,1,0:T(8,128)}, f32[2,2,192,768]{3,2,1,0:T(8,128)}, f32[2,2,192,768]{3,2,1,0:T(8,128)}) async-done(((f32[2,2,192,768]{3,2,1,0:T(8,128)}, f32[2,2,192,768]{3,2,1,0:T(8,128)}, f32[2,2,192,768]{3,2,1,0:T(8,128)}, f32[2,2,192,768]{3,2,1,0:T(8,128)}), (f32[2,2,192,768]{3,2,1,0:T(8,128)}, f32[2,2,192,768]{3,2,1,0:T(8,128)}, ...) | async-done | bytes 9437200 | tf_op jit(solution)/shard_map/psum | solution.py:57
  1247.0 77.5 %all-reduce.1 = (f32[6,768]{1,0:T(8,128)S(1)}, f32[2,3]{0,1:T(4,128)S(1)}, f32[2,3]{0,1:T(4,128)S(1)}, f32[2,3,384]{2,1,0:T(4,128)S(1)}, f32[2]{0:T(128)S(1)}, /...) all-reduce(f32[6,768]{1,0:T(8,128)S(1)} %add.350, ...), channel_id=1, replica_groups=mesh['dp'=4,'seq'=4,'tensor'=2] {'dp','seq'}, use_global_device_ids=true, to_apply=%region_60.0 | all-reduce | flops 10772 | bytes 86176 | tf_op jit(solution)/shard_map/psum | solution.py:291
  (660 shorter events, 419.8 us)
Async XLA Ops:
  7.2 78.2 %all-gather.4.cloned.1.call-start = ((), (), s32[]{:S(2)}) async-start(), calls=%async_computation.10 | async-start | bytes 3760128 | tf_op jit(solution)/shard_map/all_gather | solution.py:259
  10.8 85.5 %copy-start.178 = (f32[768]{0:T(1024)}, f32[768]{0:T(1024)S(1)}, u32[]{:S(2)}) copy-start(f32[768]{0:T(1024)S(1)} %get-tuple-element.163) | copy-start | bytes 9220
  91.9 44.7 %all-to-all-start.2 = ((bf16[3,2,2,192,384]{4,2,1,0,3:T(2,128)(2,1)}), bf16[3,2,2,192,384]{4,2,1,0,3:T(2,128)(2,1)}, u32[]{:S(2)}, u32[]{:S(2)}) async-start(bf16[3,2,2,192,384]{4,2,1,0,3:T(2,128)(2,1)} %copy.425), calls=%async_computation.2 | async-start | bytes 3538944 | tf_op jit(solution)/shard_map/all_to_all | solution.py:49
  136.6 46.8 %all-to-all-start = ((bf16[3,2,2,192,384]{4,2,1,0,3:T(2,128)(2,1)}), bf16[3,2,2,192,384]{4,2,1,0,3:T(2,128)(2,1)}, u32[]{:S(2)}, u32[]{:S(2)}) async-start(bf16[3,2,2,192,384]{4,2,1,0,3:T(2,128)(2,1)} %copy.410), calls=%async_computation | async-start | bytes 3538944 | tf_op jit(solution)/shard_map/all_to_all | solution.py:49
  141.0 95.9 %all-gather.6.cloned.1.call-start = ((), (), s32[]{:S(2)}) async-start(), calls=%async_computation.11 | async-start | bytes 1253376 | tf_op jit(solution)/shard_map/all_gather | solution.py:260
  183.3 31.8 %all-to-all-start.3 = ((bf16[1,2,8,48,384]{4,3,1,0,2:T(8,128)(2,1)}), bf16[1,2,8,48,384]{4,3,1,0,2:T(8,128)(2,1)S(1)}, u32[]{:S(2)}, u32[]{:S(2)}) async-start(bf16[1,2,8,48,384]{4,3,1,0,2:T(8,128)(2,1)} %reshape.378), calls=%async_computation.3 | async-start | bytes 1179648 | tf_op jit(solution)/shard_map/all_to_all | solution.py:53
  215.1 19.8 %all-to-all-start.1 = ((bf16[1,2,8,48,384]{4,3,1,0,2:T(8,128)(2,1)}), bf16[1,2,8,48,384]{4,3,1,0,2:T(8,128)(2,1)}, u32[]{:S(2)}, u32[]{:S(2)}) async-start(bf16[1,2,8,48,384]{4,3,1,0,2:T(8,128)(2,1)} %reshape.377), calls=%async_computation.1 | async-start | bytes 1179648 | tf_op jit(solution)/shard_map/all_to_all | solution.py:53
  220.2 50.1 %all-reduce.25.cloned.1.call-start = ((), (), s32[]{:S(2)}) async-start(), calls=%async_computation.20 | async-start | bytes 9437184 | tf_op jit(solution)/shard_map/psum | solution.py:57
  242.7 97.4 %all-reduce.23.cloned.1.call-start = ((), (), s32[]{:S(2)}) async-start(), calls=%async_computation.19 | async-start | bytes 9437184 | tf_op jit(solution)/shard_map/psum | solution.py:57
  309.6 114.9 %all-gather.8.cloned.1.call-start = ((), (), s32[]{:S(2)}) async-start(), calls=%async_computation.12 | async-start | bytes 5013504 | tf_op jit(solution)/shard_map/all_gather | solution.py:261
  311.7 188.0 %all-reduce.21.cloned.1.call-start = ((), (), s32[]{:S(2)}) async-start(), calls=%async_computation.18 | async-start | bytes 9437184 | tf_op jit(solution)/shard_map/psum | solution.py:57
  471.6 126.4 %all-reduce.19.cloned.1.call-start = ((), (), s32[]{:S(2)}) async-start(), calls=%async_computation.17 | async-start | bytes 9437184 | tf_op jit(solution)/shard_map/psum | solution.py:57
  567.4 275.5 %reduce-scatter.3.cloned.1.call-start = ((), (), s32[]{:S(2)}) async-start(), calls=%async_computation.13 | async-start | bytes 2506752 | tf_op jit(solution)/shard_map/reduce_scatter | solution.py:275
  614.8 350.6 %reduce-scatter.5.cloned.1.call-start = ((), (), s32[]{:S(2)}) async-start(), calls=%async_computation.14 | async-start | bytes 10027008 | tf_op jit(solution)/shard_map/reduce_scatter | solution.py:276
  635.2 24.9 %all-to-all-start.4 = ((bf16[1,2,2,192,384]{4,2,1,0,3:T(2,128)(2,1)}), bf16[1,2,2,192,384]{4,2,1,0,3:T(2,128)(2,1)}, u32[]{:S(2)}, u32[]{:S(2)}) async-start(bf16[1,2,2,192,384]{4,2,1,0,3:T(2,128)(2,1)} %copy.447), calls=%async_computation.4 | async-start | bytes 1179648 | tf_op jit(solution)/shard_map/all_to_all | solution.py:49
  660.2 36.4 %all-to-all-start.6 = ((bf16[1,2,2,192,384]{4,2,1,0,3:T(2,128)(2,1)}), bf16[1,2,2,192,384]{4,2,1,0,3:T(2,128)(2,1)}, u32[]{:S(2)}, u32[]{:S(2)}) async-start(bf16[1,2,2,192,384]{4,2,1,0,3:T(2,128)(2,1)} %copy.468), calls=%async_computation.6 | async-start | bytes 1179648 | tf_op jit(solution)/shard_map/all_to_all | solution.py:49
  696.6 52.2 %all-to-all-start.5 = ((bf16[3,2,8,48,384]{4,3,1,0,2:T(8,128)(2,1)}), bf16[3,2,8,48,384]{4,3,1,0,2:T(8,128)(2,1)}, u32[]{:S(2)}, u32[]{:S(2)}) async-start(bf16[3,2,8,48,384]{4,3,1,0,2:T(8,128)(2,1)} %copy.458), calls=%async_computation.5 | async-start | bytes 3538944 | tf_op jit(solution)/shard_map/all_to_all | solution.py:53
  748.9 48.2 %all-to-all-start.7 = ((bf16[3,2,8,48,384]{4,3,1,0,2:T(8,128)(2,1)}), bf16[3,2,8,48,384]{4,3,1,0,2:T(8,128)(2,1)}, u32[]{:S(2)}, u32[]{:S(2)}) async-start(bf16[3,2,8,48,384]{4,3,1,0,2:T(8,128)(2,1)} %copy.479), calls=%async_computation.7 | async-start | bytes 3538944 | tf_op jit(solution)/shard_map/all_to_all | solution.py:53
  753.3 443.8 %all-reduce.15.cloned.1.call-start = ((), (), s32[]{:S(2)}) async-start(), calls=%async_computation.15 | async-start | bytes 14155776
  822.9 417.6 %all-reduce.17.cloned.1.call-start = ((), (), s32[]{:S(2)}) async-start(), calls=%async_computation.16 | async-start | bytes 18874368 | tf_op jit(solution)/shard_map/psum | solution.py:57
  840.8 361.5 %copy-start.185 = (f32[2,48]{1,0:T(2,128)S(1)}, f32[2,48]{1,0:T(2,128)}, u32[]{:S(2)}) copy-start(f32[2,48]{1,0:T(2,128)} %param.27) | copy-start | bytes 1156
  840.9 361.5 %copy-start.186 = (f32[2,48]{1,0:T(2,128)S(1)}, f32[2,48]{1,0:T(2,128)}, u32[]{:S(2)}) copy-start(f32[2,48]{1,0:T(2,128)} %param.24) | copy-start | bytes 1156
  1202.5 137.3 %copy-start.177 = (f32[2,48]{1,0:T(2,128)}, f32[2,48]{1,0:T(2,128)S(1)}, u32[]{:S(2)}) copy-start(f32[2,48]{1,0:T(2,128)S(1)} %get-tuple-element.264) | copy-start | bytes 1156
  1202.5 138.1 %copy-start.176 = (f32[2,48]{1,0:T(2,128)}, f32[2,48]{1,0:T(2,128)S(1)}, u32[]{:S(2)}) copy-start(f32[2,48]{1,0:T(2,128)S(1)} %get-tuple-element.239) | copy-start | bytes 1156
  (196 other events, 1700.5 us)
Sparse Core Ops, SparseCore 0:
  11.5 73.9 all-gather.3
  145.2 66.7 all-gather.5
  242.8 27.3 all-reduce.24
  309.7 30.3 all-reduce.22
  342.9 81.6 all-gather.7
  471.7 27.8 all-reduce.20
  567.6 30.3 all-reduce.18
  614.9 158.1 reduce-scatter.2
  780.4 184.9 reduce-scatter.4
  971.5 225.5 all-reduce.14
  1200.5 40.0 all-reduce.16
where the time goes:
time: 1360 us; the launch traced here: 1350 us
  waiting for transfers between devices  768 us (56%)
  matrix products  178 us (13%)
  local copies, waits for them, and re-layouts  154 us (11%)
  other arithmetic  112 us (8%)
  blocking collectives  80 us (6%)
  starting transfers between devices  38.5 us (3%)
  between operations  18 us (1%)
    unnamed x12, waiting for transfers between devices  230 us
    psum x5, waiting for transfers between devices, tensor_total(): return lax.psum(partial_term, 'tensor')  142 us
    reduce_scatter x1, waiting for transfers between devices, per_device(): lax.psum_scatter(weight_grads[2], ('dp', 'seq'), scatter_dimension=1, til...  121 us
    psum x1, blocking collectives, per_device(): lax.psum((col_part[0], col_part[1], col_part[2], section_one[3], section_...  77.5 us
    all_gather x1, waiting for transfers between devices, per_device(): lax.all_gather(shards[2], ('dp', 'seq'), axis=1, tiled=True)  76.2 us
    all_gather x1, waiting for transfers between devices, per_device(): lax.all_gather(shards[0], ('dp', 'seq'), axis=2, tiled=True)  71.7 us
    all_to_all x4, waiting for transfers between devices, to_places(): lax.all_to_all(stacked, 'seq', split_axis=3, concat_axis=2, tiled=True)  68 us
    all_to_all x4, waiting for transfers between devices, to_frames(): lax.all_to_all(stacked, 'seq', split_axis=2, concat_axis=3, tiled=True)  57.8 us
  transfers between devices with their start and end apart: 19, of which 15 were waited for; matrix products, arithmetic and copies ran while one was open for 17% of the time, Pallas kernels for 0%

commit v1 on v0

--- a/solution.py
+++ b/solution.py
@@ -1,6 +1,8 @@
 import jax
 import jax.numpy as jnp
 from jax import lax
+from jax.experimental import pallas as pl
+from jax.experimental.pallas import tpu as pltpu
 from jax.sharding import PartitionSpec as P
 
 HEAD_DIM = 64
@@ -358,6 +360,1565 @@
     )
 
 
+MESH_ID = pl.DeviceIdType.MESH
+BF = jnp.bfloat16
+F32 = jnp.float32
+NEG = -1e30
+SQRT_HALF = 0.7071067811865476
+INV_SQRT_2PI = 0.3989422804014327
+
+
+def nn(a, b):
+    return lax.dot_general(a, b, (((1,), (0,)), ((), ())), preferred_element_type=F32)
+
+
+def nt(a, b):
+    return lax.dot_general(a, b, (((1,), (1,)), ((), ())), preferred_element_type=F32)
+
+
+def tn(a, b):
+    return lax.dot_general(a, b, (((0,), (0,)), ((), ())), preferred_element_type=F32)
+
+
+def flat(values):
+    return values.reshape(-1, values.shape[-1])
+
+
+def ln_stats(v):
+    centred = v - jnp.mean(v, -1, keepdims=True)
+    rstd = lax.rsqrt(jnp.mean(centred * centred, -1, keepdims=True) + EPS)
+    return centred * rstd, rstd
+
+
+def ln_rows(v, gain, bias):
+    return ln_stats(v)[0] * gain + bias
+
+
+def ln_back(v, gain, dh):
+    hat, rstd = ln_stats(v)
+    g = dh * gain
+    dv = rstd * (
+        g - jnp.mean(g, -1, keepdims=True) - hat * jnp.mean(g * hat, -1, keepdims=True)
+    )
+    return dv, dh * hat
+
+
+def gelu_pair(z):
+    size = jnp.abs(z)
+    bell = jnp.exp(-0.5 * z * z)
+    u = 1.0 / (1.0 + (0.3275911 * SQRT_HALF) * size)
+    poly = u * (
+        0.254829592
+        + u * (-0.284496736 + u * (1.421413741 + u * (-1.453152027 + u * 1.061405429)))
+    )
+    tail = 0.5 * poly * bell
+    below = jnp.where(z < 0.0, tail, 1.0 - tail)
+    return below, z * bell * INV_SQRT_2PI
+
+
+def by_heads(values, factor):
+    lane = lax.broadcasted_iota(jnp.int32, (1, 2 * HEAD_DIM), 1)
+    first = (lane < HEAD_DIM).astype(F32)
+    return jnp.concatenate(
+        [values * (first * factor).astype(BF), values * ((1.0 - first) * factor).astype(BF)], 0
+    )
+
+
+def softmax_rows(s, keep):
+    if keep is not None:
+        s = jnp.where(keep, s, NEG)
+    ex = jnp.exp(s - jnp.max(s, 0, keepdims=True))
+    return ex * (1.0 / jnp.sum(ex, 0, keepdims=True))
+
+
+def by_head_lanes(both, factor=None):
+    n = both.shape[0] // 2
+    first = lax.broadcasted_iota(jnp.int32, (1, 2 * HEAD_DIM), 1) < HEAD_DIM
+    out = jnp.where(first, both[:n], both[n:])
+    return (out if factor is None else out * factor).astype(BF)
+
+
+def attn_forward(qs, ks, vs, keep):
+    scores = [nt(k, by_heads(q, SCALE)) for q, k in zip(qs, ks)]
+    probs = [softmax_rows(s, keep).astype(BF) for s in scores]
+    return [by_head_lanes(tn(p, v)) for p, v in zip(probs, vs)]
+
+
+def attn_backward(qs, ks, vs, gs, keep):
+    qms, gms = [by_heads(q, SCALE) for q in qs], [by_heads(g, 1.0) for g in gs]
+    scores = [nt(k, qm) for k, qm in zip(ks, qms)]
+    dps = [nt(v, gm) for v, gm in zip(vs, gms)]
+    probs = [softmax_rows(s, keep) for s in scores]
+    dss = [
+        (p * (dp - jnp.sum(p * dp, 0, keepdims=True))).astype(BF) for p, dp in zip(probs, dps)
+    ]
+    lows = [p.astype(BF) for p in probs]
+    dqs = [by_head_lanes(tn(ds, k), SCALE) for ds, k in zip(dss, ks)]
+    dks = [nn(ds, qm).astype(BF) for ds, qm in zip(dss, qms)]
+    dvs = [nn(p, gm).astype(BF) for p, gm in zip(lows, gms)]
+    return dqs, dks, dvs
+
+
+def head_lanes(first, count):
+    return [slice(128 * j, 128 * (j + 1)) for j in range(first, first + count)]
+
+
+def same_patch(rows, keys, group):
+    a = lax.broadcasted_iota(jnp.int32, (rows, keys), 0)
+    b = lax.broadcasted_iota(jnp.int32, (rows, keys), 1)
+    return lax.rem(a, group) == lax.rem(b, group)
+
+
+def remote(src, dst, send_sem, recv_sem, device):
+    return pltpu.make_async_remote_copy(
+        src_ref=src,
+        dst_ref=dst,
+        send_sem=send_sem,
+        recv_sem=recv_sem,
+        device_id=device,
+        device_id_type=MESH_ID,
+    )
+
+
+def places():
+    d, z, t = lax.axis_index("dp"), lax.axis_index("seq"), lax.axis_index("tensor")
+    y, x = lax.div(d, 2), lax.rem(d, 2)
+    across_x = (2 * y + 1 - x, z, t)
+    across_y = (2 * (1 - y) + x, z, t)
+    other = (d, z, 1 - t)
+    along = [(d, lax.rem(z + j, NZ), t) for j in range(1, NZ)]
+    return d, y, x, z, t, across_x, across_y, other, along
+
+
+def add(total, part):
+    total[...] = total[...] + part[...]
+
+
+def greet(devices):
+    barrier = pltpu.get_barrier_semaphore()
+    for device in devices:
+        pl.semaphore_signal(barrier, inc=1, device_id=device, device_id_type=MESH_ID)
+    pl.semaphore_wait(barrier, len(devices))
+
+
+NZ = 4
+LINES = 96
+
+
+def wide(pair):
+    return jnp.concatenate([flat(pair[0]), flat(pair[1])], 1)
+
+
+def lines(ref, i):
+    per = ref.shape[1] // LINES
+    if per == 1:
+        return (i, slice(None), slice(None))
+    start = pl.multiple_of(lax.rem(i, per) * LINES, LINES)
+    return (lax.div(i, per), pl.ds(start, LINES), slice(None))
+
+
+def forward_kernel(
+    clips,
+    cot,
+    qkvw,
+    outw,
+    ffnw,
+    norm,
+    counts,
+    wa_o,
+    xt_o,
+    h0_o,
+    qkv0_o,
+    os_o,
+    y1_o,
+    h1_o,
+    qkv1_o,
+    o1_o,
+    dy2_o,
+    lo_o,
+    gf_o,
+    block_o,
+    ng_o,
+    w,
+    xt,
+    xs,
+    h0,
+    qkv0,
+    ot,
+    os_,
+    y1,
+    h1,
+    qkv1,
+    o1,
+    h3,
+    ct,
+    h3a,
+    ea,
+    h3t,
+    et,
+    acc,
+    dh3,
+    act,
+    dz,
+    wf,
+    r1,
+    r2,
+    z1s,
+    z1r,
+    z2s,
+    z3s,
+    zpr,
+    x1s,
+    x1r,
+    x2s,
+    x2r,
+    ks,
+    kr,
+    ts,
+    tr,
+    tl,
+    es,
+    er,
+    el,
+    sv,
+    fs,
+    fv,
+    g2s,
+    g2r,
+    g3s,
+    g3r,
+):
+    d, y, x, z, t, across_x, across_y, other, along = places()
+    greet([across_x, across_y, other] + along)
+
+    fr = clips.shape[1]
+    half = clips.shape[2] // 2
+    frames = NZ * fr
+    fh = frames // 2
+    mine = pl.ds(pl.multiple_of(t * half, half), half)
+
+    def tokens_in(src, dst, which):
+        here = dst.at[pl.ds(z * fr, fr)]
+        own = pltpu.make_async_copy(src.at[z, :, mine], here, tl.at[which])
+        own.start()
+        copies = []
+        for j, device in enumerate(along):
+            copy = remote(
+                src.at[device[1], :, mine], here, ts.at[which, j], tr.at[which, j], device
+            )
+            copy.start()
+            copies.append(copy)
+        return own, copies
+
+    def tokens_wait(started):
+        started[0].wait()
+        for copy in started[1]:
+            copy.wait_recv()
+
+    def to_frames_half(src, dst, which):
+        own = pltpu.make_async_copy(src.at[pl.ds(t * fh, fh)], dst.at[:, mine], el.at[which])
+        own.start()
+        copy = remote(
+            src.at[pl.ds((1 - t) * fh, fh)], dst.at[:, mine], es.at[which], er.at[which], other
+        )
+        copy.start()
+        return own, copy
+
+    def exchange_wait(started):
+        started[0].wait()
+        started[1].wait_recv()
+
+    pending = []
+
+    def save(src, dst):
+        copy = pltpu.make_async_copy(src, dst, sv.at[len(pending)])
+        copy.start()
+        pending.append(copy)
+        return copy
+
+    for i in range(2):
+        for s in range(3):
+            w[4 * i + s, t, y, x, z] = qkvw[i, s].astype(BF)
+        w[4 * i + 3, t, y, x, z] = outw[i].astype(BF)
+        for c in range(4):
+            wf[2 * c + i, y, x, z] = ffnw[i, :, 384 * c : 384 * (c + 1)].astype(BF)
+
+    inner = jnp.logical_or(z == 1, z == 2)
+    near, far = 2 * lax.div(z, 2), 2 - 2 * lax.div(z, 2)
+    partner, over = (d, z + 1 - 2 * lax.rem(z, 2), t), (d, NZ - 1 - z, t)
+
+    def own(u):
+        return w.at[u, t] if u < 8 else wf.at[u - 8]
+
+    def z_one(u):
+        ref = own(u).at[y, x, z]
+        return remote(ref, ref, z1s.at[u], z1r.at[u], partner)
+
+    def z_two(u):
+        ref = own(u).at[y, x, pl.ds(near, 2)]
+        return remote(ref, ref, z2s.at[u], zpr.at[u], over)
+
+    def z_three(u):
+        ref = own(u).at[y, x, pl.ds(far, 2)]
+        return remote(ref, ref, z3s.at[u], zpr.at[u], partner)
+
+    def plane_one(u, i):
+        ref = own(u).at[y, x]
+        return remote(ref, ref, x1s.at[u], x1r.at[u], across_y if i else across_x)
+
+    def plane_two(u, i):
+        ref = own(u).at[:, x] if i else own(u).at[y]
+        return remote(ref, ref, x2s.at[u], x2r.at[u], across_x if i else across_y)
+
+    def to_core(u):
+        ref = w.at[u, t]
+        return remote(ref, ref, ks.at[u], kr.at[u], other)
+
+    def send_z1(p):
+        for u in (2 * p, 2 * p + 1):
+            z_one(u).start()
+
+    def send_z2(p):
+        for u in (2 * p, 2 * p + 1):
+            z_one(u).wait_recv()
+
+        @pl.when(inner)
+        def _():
+            for u in (2 * p, 2 * p + 1):
+                z_two(u).start()
+
+    def send_z3(p):
+        @pl.when(inner)
+        def _():
+            for u in (2 * p, 2 * p + 1):
+                z_three(u).wait_recv()
+                z_three(u).start()
+
+    def send_one(p):
+        @pl.when(jnp.logical_not(inner))
+        def _():
+            for u in (2 * p, 2 * p + 1):
+                z_three(u).wait_recv()
+
+        for i in range(2):
+            plane_one(2 * p + i, i).start()
+
+    def send_two(p):
+        for i in range(2):
+            plane_one(2 * p + i, i).wait_recv()
+            plane_two(2 * p + i, i).start()
+
+    def send_core(p):
+        for i in range(2):
+            plane_two(2 * p + i, i).wait_recv()
+            to_core(2 * p + i).start()
+
+    def need(p):
+        for i in range(2):
+            u = 2 * p + i
+            if u < 8:
+                to_core(u).wait_recv()
+                to_core(u).wait_send()
+            else:
+                plane_two(u, i).wait_recv()
+            plane_one(u, i).wait_send()
+            plane_two(u, i).wait_send()
+            z_one(u).wait_send()
+
+        @pl.when(inner)
+        def _():
+            for u in (2 * p, 2 * p + 1):
+                z_two(u).wait_send()
+                z_three(u).wait_send()
+
+    def run(*events):
+        for stage, p in events:
+            stage(p)
+
+    def at_step(i, k, *events):
+        @pl.when(i == k)
+        def _():
+            run(*events)
+
+    for stage in (send_z1, send_z2):
+        for p in range(4):
+            stage(p)
+    run((send_z3, 0), (send_z3, 1))
+    x_in = tokens_in(clips, xt, 0)
+    run((send_z3, 2), (send_z3, 3), (send_one, 0), (send_one, 1))
+    for p in range(4, 8):
+        send_z1(p)
+    run((send_one, 2), (send_two, 0), (send_two, 1), (send_core, 0), (send_one, 3))
+    run((send_two, 2), (send_core, 1))
+    need(0)
+    need(1)
+
+    gain, bias = norm[0:1, :], norm[3:4, :]
+
+    def tokens_part(k, carry):
+        base = lax.rem(z - k + NZ, NZ) * fr
+
+        @pl.when(k == 0)
+        def _():
+            x_in[0].wait()
+
+        @pl.when(k > 0)
+        def _():
+            j = jnp.maximum(k - 1, 0)
+            here = xt.at[pl.ds(0, fr)]
+            remote(here, here, ts.at[0, j], tr.at[0, j], other).wait_recv()
+
+        for f in range(fr):
+            h0[base + f] = ln_rows(xt[base + f].astype(F32), gain, bias).astype(BF)
+        left = flat(h0[pl.ds(base, fr)])
+        for s in range(3):
+            part = nn(left, wide(w.at[s])).astype(BF)
+            qkv0[s, pl.ds(base, fr)] = part.reshape((fr,) + h0.shape[1:])
+        at_step(k, 0, (send_z2, 4), (send_z2, 5))
+        at_step(k, 2, (send_z2, 6), (send_z2, 7), (send_z3, 4), (send_z3, 5))
+        return carry
+
+    lax.fori_loop(0, NZ, tokens_part, 0)
+    x_ex = to_frames_half(xt, xs, 0)
+    save(xt, xt_o)
+    save(h0, h0_o)
+    save(qkv0, qkv0_o)
+    run((send_two, 3), (send_one, 4), (send_core, 2))
+
+    def project(src, dst, u, s):
+        lead = src.shape[0] // 2
+
+        def block(i, carry):
+            rows = pl.ds(i * lead, lead)
+            part = nn(flat(src[rows]), wide(w.at[u])).astype(BF)
+            dst[s, rows] = part.reshape((lead,) + src.shape[1:])
+            return carry
+
+        lax.fori_loop(0, 2, block, 0)
+
+    keep = same_patch(frames * 16, 2 * frames * 16, 16)
+
+    def temporal(b, carry):
+        rows = pl.ds(pl.multiple_of(b * 16, 16), 16)
+        for j in range(0, 6, 3):
+            group = head_lanes(j, 3)
+            parts = [[flat(qkv0[s, :, rows, at]) for at in group] for s in range(3)]
+            for at, out in zip(group, attn_forward(*parts, keep)):
+                ot[:, rows, at] = out.reshape((frames, 16, 128))
+        at_step(b, 1, (send_z3, 6), (send_z3, 7))
+        at_step(b, 3, (send_one, 5), (send_core, 3))
+        at_step(b, 5, (send_two, 4))
+        return carry
+
+    lax.fori_loop(0, half // 16, temporal, 0)
+    c_in = tokens_in(cot, ct, 1)
+    o_ex = to_frames_half(ot, os_, 1)
+
+    exchange_wait(x_ex)
+    exchange_wait(o_ex)
+    mixed_saved = save(os_, os_o)
+    gain1, bias1 = norm[1:2, :], norm[4:5, :]
+
+    def branch_sum(mixed, base, total, u, normed, gain, bias):
+        def block(i, carry):
+            two_frames = pl.ds(2 * i, 2)
+            part = nt(flat(mixed[two_frames]), wide(w.at[u]))
+            total[two_frames] = base[two_frames].astype(F32) + part.reshape(
+                (2,) + mixed.shape[1:]
+            )
+            return carry
+
+        lax.fori_loop(0, fh // 2, block, 0)
+
+        def rescale(i, carry):
+            at = lines(total, i)
+            normed[at] = ln_rows(total[at], gain, bias).astype(BF)
+            return carry
+
+        lax.fori_loop(0, frames * half // LINES, rescale, 0, unroll=2)
+
+    branch_sum(os_, xs, y1, 3, h1, gain1, bias1)
+    y1_saved = save(y1, y1_o)
+    h1_saved = save(h1, h1_o)
+    run((send_one, 6), (send_two, 5))
+    need(2)
+    project(h1, qkv1, 4, 0)
+    project(h1, qkv1, 5, 1)
+    need(3)
+    project(h1, qkv1, 6, 2)
+    save(qkv1, qkv1_o)
+    for u in range(8):
+        save(w.at[u], wa_o.at[u])
+
+    def spatial(b, carry):
+        for j in range(0, 6, 2):
+            group = head_lanes(j, 2)
+            parts = [[qkv1[s, b, :, at] for at in group] for s in range(3)]
+            for at, out in zip(group, attn_forward(*parts, None)):
+                o1[b, :, at] = out
+        at_step(b, 1, (send_one, 7))
+        at_step(b, 3, (send_two, 6))
+        return carry
+
+    lax.fori_loop(0, fh, spatial, 0)
+    save(o1, o1_o)
+    gain2, bias2 = norm[2:3, :], norm[5:6, :]
+
+    y1_saved.wait()
+    branch_sum(o1, y1, y1, 7, h3, gain2, bias2)
+    ours, others = pl.ds(t * fh, fh), pl.ds((1 - t) * fh, fh)
+
+    def to_other(src, dst, which):
+        copy = remote(src, dst, fs.at[which], fv.at[which], other)
+        copy.start()
+        return copy
+
+    mixed_saved.wait()
+    h3_ex = to_other(h3, h3a.at[ours], 0)
+    h3_own = pltpu.make_async_copy(h3, h3a.at[ours], el.at[2])
+    h3_own.start()
+    tokens_wait(c_in)
+    c_ex = to_other(ct, ea.at[:, mine], 1)
+    c_own = pltpu.make_async_copy(ct, ea.at[:, mine], el.at[3])
+    c_own.start()
+    run((send_two, 7),)
+    acc[...] = jnp.zeros_like(acc)
+    dh3[...] = jnp.zeros_like(dh3)
+    h3_own.wait()
+    h3_ex.wait()
+
+    def turn(src, dst):
+        for i in range(2):
+            block = slice(i * fh, (i + 1) * fh)
+            lanes = slice(i * dst.shape[1] // 2, (i + 1) * dst.shape[1] // 2)
+            dst[:, lanes] = flat(src[block]).T
+
+    turn(h3a, h3t)
+    c_own.wait()
+    c_ex.wait()
+    on = jnp.where(z < counts[0], 1.0, 0.0)
+
+    def prepare(i, carry):
+        ea[i] = (ea[i].astype(F32) * on).astype(BF)
+        return carry
+
+    lax.fori_loop(0, frames, prepare, 0)
+    turn(ea, et)
+
+    def give_one_copy(r):
+        src = wf.at[r, :, 1 - x] if r % 2 else wf.at[r, 1 - y]
+        return remote(src, r1.at[r], g2s.at[r], g2r.at[r], across_x if r % 2 else across_y)
+
+    def give_two_copy(r):
+        src = wf.at[r, 1 - y, x] if r % 2 else wf.at[r, y, 1 - x]
+        return remote(src, r2.at[r], g3s.at[r], g3r.at[r], across_y if r % 2 else across_x)
+
+    def give_one(r):
+        give_one_copy(r).start()
+
+    def give_two(r):
+        give_one_copy(r).wait_recv()
+        total, part = wf.at[r], r1.at[r]
+        add(total.at[(1 - y, x) if r % 2 else (y, 1 - x)], part.at[1 - y if r % 2 else 1 - x])
+        give_two_copy(r).start()
+        add(total.at[y, x], part.at[y if r % 2 else x])
+
+    def give_last(r):
+        give_two_copy(r).wait_recv()
+        block = wf.at[r, y, x]
+        add(block, r2.at[r])
+        save(block, block_o.at[r])
+
+    def hidden_half(c, carry):
+        for k in range(2):
+
+            @pl.when(c == k)
+            def _():
+                need(4 + 2 * k)
+                need(5 + 2 * k)
+
+        def side(first):
+            return jnp.concatenate([flat(wf[4 * c + first]), flat(wf[4 * c + first + 2])], 1)
+
+        def some_tokens(i, carry):
+            f0, f1 = side(0), side(1)
+            here = pl.ds(2 * i, 2)
+            rows = pl.ds(pl.multiple_of(i * 4 * half, 4 * half), 4 * half)
+            pre = nn(flat(h3a[here]), f0)
+            below, slope = gelu_pair(pre)
+            active = (pre * below).astype(BF)
+            act[rows, :] = active
+            back = (nn(flat(ea[here]), f1) * (below + slope)).astype(BF)
+            dz[rows, :] = back
+            shape = (2,) + ea.shape[1:]
+            acc[here] += nt(active, f1).reshape(shape)
+            dh3[here] += nt(back, f0).reshape(shape)
+            return carry
+
+        lax.fori_loop(0, frames // 2, some_tokens, 0)
+        for first, left, right in ((0, h3t, dz), (1, et, act)):
+
+            def some_rows(i, carry):
+                rows = pl.ds(pl.multiple_of(i * 384, 384), 384)
+                total = nn(left[rows, :], right[...]).astype(BF)
+                for k in range(2):
+                    part = total[:, 384 * k : 384 * (k + 1)]
+                    wf[4 * c + first + 2 * k, i] = part.reshape(wf.shape[2:])
+                return carry
+
+            lax.fori_loop(0, 2, some_rows, 0)
+        at_step(c, 0, *[(give_one, r) for r in range(4)])
+        return carry
+
+    lax.fori_loop(0, 2, hidden_half, 0)
+    save(wf.at[pl.ds(4, 4)], gf_o)
+    for i in range(fh):
+        h3a[(1 - t) * fh + i] = acc[(1 - t) * fh + i].astype(BF)
+    out_ex = to_other(h3a.at[others], xs, 2)
+    for i in range(fh):
+        ea[(1 - t) * fh + i] = dh3[(1 - t) * fh + i].astype(BF)
+    dh_ex = to_other(ea.at[others], os_, 3)
+    for r in range(4):
+        give_two(r)
+
+    def finish(i, sums):
+        at = lines(y1, i)
+        here = (t * fh + at[0],) + at[1:]
+        v = y1[at]
+        up = dh3[here] + os_[at].astype(F32)
+        h1[at] = (v + (acc[here] + xs[at].astype(F32))).astype(BF)
+        dv, dg = ln_back(v, gain2, up)
+        dh3[here] = ea[here].astype(F32) + dv
+        return (
+            sums[0] + jnp.sum(dg, 0, keepdims=True),
+            sums[1] + jnp.sum(up, 0, keepdims=True),
+        )
+
+    h1_saved.wait()
+    out_ex.wait()
+    dh_ex.wait()
+    zero = jnp.zeros((1, norm.shape[1]), F32)
+    dg, db = lax.fori_loop(0, frames * half // LINES, finish, (zero, zero), unroll=2)
+    ng_o[...] = jnp.zeros_like(ng_o)
+    ng_o[2:3, :] = dg
+    ng_o[5:6, :] = db
+    save(h1, lo_o)
+    save(dh3.at[ours], dy2_o)
+    for r in range(4):
+        give_last(r)
+    for r in range(4):
+        give_one_copy(r).wait_send()
+        give_two_copy(r).wait_send()
+    for started in (x_in, c_in):
+        for copy in started[1]:
+            copy.wait_send()
+    for started in (x_ex, o_ex):
+        started[1].wait_send()
+    for copy in pending:
+        if all(copy is not early for early in (mixed_saved, y1_saved, h1_saved)):
+            copy.wait()
+
+
+RS_ORDER = [8, 9, 10, 11, 12, 13, 14, 15, 7, 4, 5, 6, 3, 0, 1, 2]
+GROUPS = [[0, 1], [2, 3], [4, 5], [6, 7], [8], [9, 10], [11, 12], [13, 14], [15]]
+
+
+def backward_kernel(
+    wa_i,
+    xt_i,
+    h0_i,
+    qkv0_i,
+    os_i,
+    y1_i,
+    h1_i,
+    qkv1_i,
+    o1_i,
+    dy2_i,
+    lo_i,
+    gf_i,
+    block_i,
+    norm,
+    ng_i,
+    qkv_row,
+    out_row,
+    ffn_row,
+    gsum,
+    row_o,
+    pack_o,
+    lo_t,
+    lo_o,
+    gi_o,
+    wa,
+    xt,
+    h0,
+    qkv0,
+    os_,
+    y1,
+    h1,
+    qkv1,
+    o1,
+    dy,
+    e,
+    et,
+    ht,
+    do,
+    e0,
+    gt,
+    dh,
+    pf,
+    block,
+    tg,
+    gr,
+    r1,
+    r2,
+    r3,
+    ld,
+    pd,
+    ks,
+    kr,
+    x1s,
+    x1r,
+    x2s,
+    x2r,
+    z1s,
+    z1r,
+    z2s,
+    z2r,
+    z3s,
+    z3r,
+    es,
+    er,
+    el,
+    ts,
+    tr,
+    tl,
+    ss,
+    sr,
+    as_,
+    ar,
+    row_in,
+    pack_in,
+    held,
+):
+    d, y, x, z, t, across_x, across_y, other, along = places()
+    greet([across_x, across_y, (3 - d, z, t), other] + along)
+
+    half = xt.shape[1]
+    frames = xt.shape[0]
+    fh = frames // 2
+    fr = frames // NZ
+    mine = pl.ds(pl.multiple_of(t * half, half), half)
+    theirs = pl.ds(pl.multiple_of((1 - t) * half, half), half)
+
+    loads = {}
+
+    def load(name, src, dst):
+        loads[name] = pltpu.make_async_copy(src, dst, ld.at[len(loads)])
+        loads[name].start()
+
+    def own_part(r):
+        return pltpu.make_async_copy(gf_i.at[r - 4], pf.at[r - 4], pd.at[r])
+
+    def block_in(r):
+        return pltpu.make_async_copy(block_i.at[r], block.at[r], pd.at[r])
+
+    def halves(r):
+        return tg.at[r - 13] if r >= 13 else wa.at[RS_ORDER[r]]
+
+    def grad_ref(r):
+        return pf.at[r - 4] if r < 8 else halves(r).at[t]
+
+    def block_ref(r):
+        return block.at[r] if r < 4 else grad_ref(r).at[y, x]
+
+    inner = jnp.logical_or(z == 1, z == 2)
+    near, far = 2 * lax.div(z, 2), 2 - 2 * lax.div(z, 2)
+    pair = z + 1 - 2 * lax.rem(z, 2)
+    partner, over = (d, pair, t), (d, NZ - 1 - z, t)
+
+    def core_copy(r):
+        return remote(halves(r).at[1 - t], gr.at[r - 8], ks.at[r], kr.at[r], other)
+
+    def one_copy(r):
+        total = grad_ref(r)
+        src = total.at[:, 1 - x] if r % 2 else total.at[1 - y]
+        device = across_x if r % 2 else across_y
+        return remote(src, r1.at[r - 4], x1s.at[r], x1r.at[r], device)
+
+    def two_copy(r):
+        total = grad_ref(r)
+        src = total.at[1 - y, x] if r % 2 else total.at[y, 1 - x]
+        device = across_y if r % 2 else across_x
+        return remote(src, r2.at[r - 4], x2s.at[r], x2r.at[r], device)
+
+    def send_core(rs):
+        for r in rs:
+            core_copy(r).start()
+
+    def send_one(rs):
+        for r in rs:
+            if r < 8:
+                own_part(r).wait()
+                one_copy(r).start()
+                continue
+            core_copy(r).wait_recv()
+            total, part = grad_ref(r), gr.at[r - 8]
+            away = [(i, 1 - x) if r % 2 else (1 - y, i) for i in range(2)]
+            keep = [(i, x) if r % 2 else (y, i) for i in range(2)]
+            for at in away:
+                add(total.at[at], part.at[at])
+            one_copy(r).start()
+            for at in keep:
+                add(total.at[at], part.at[at])
+
+    def send_two(rs):
+        for r in rs:
+            one_copy(r).wait_recv()
+            total, part = grad_ref(r), r1.at[r - 4]
+            add(total.at[(1 - y, x) if r % 2 else (y, 1 - x)], part.at[1 - y if r % 2 else 1 - x])
+            two_copy(r).start()
+            add(total.at[y, x], part.at[y if r % 2 else x])
+
+    def z_in(r):
+        src = block_ref(r).at[pl.ds(far, 2)]
+        return remote(src, r3.at[r, pl.ds(0, 2)], z1s.at[r], z1r.at[r], partner)
+
+    def z_across(r):
+        src = block_ref(r).at[pl.ds(far, 2)]
+        return remote(src, r3.at[r, pl.ds(2, 2)], z2s.at[r], z2r.at[r], over)
+
+    def z_pair(r):
+        return remote(
+            block_ref(r).at[pair], r3.at[r, 4], z3s.at[r], z3r.at[r], partner
+        )
+
+    def z_direct(r):
+        sems = ((z1s, z1r), (z2s, z2r), (z3s, z3r))
+        return [
+            remote(block_ref(r).at[device[1]], r3.at[r, j], ss.at[r], rr.at[r], device)
+            for j, (device, (ss, rr)) in enumerate(zip(along, sems))
+        ]
+
+    def send_in(rs):
+        for r in rs:
+            if r < 4:
+                block_in(r).wait()
+            else:
+                two_copy(r).wait_recv()
+                add(block_ref(r), r2.at[r - 4])
+
+        for r in rs:
+            if r >= 13:
+                for copy in z_direct(r):
+                    copy.start()
+        if rs[0] < 13:
+
+            @pl.when(jnp.logical_not(inner))
+            def _():
+                for r in rs:
+                    z_in(r).start()
+
+    def send_across(rs):
+        @pl.when(inner)
+        def _():
+            for r in rs:
+                z_in(r).wait_recv()
+                add(block_ref(r).at[pl.ds(far, 2)], r3.at[r, pl.ds(0, 2)])
+                z_across(r).start()
+
+    def send_pair(rs):
+        @pl.when(inner)
+        def _():
+            for r in rs:
+                z_across(r).wait_recv()
+                add(block_ref(r).at[pl.ds(near, 2)], r3.at[r, pl.ds(2, 2)])
+
+        for r in rs:
+            z_pair(r).start()
+
+    lane = lax.broadcasted_iota(jnp.int32, row_o.shape, 1)
+    row_o[...] = jnp.zeros_like(row_o)
+    pack_o[...] = jnp.zeros_like(pack_o)
+
+    def settle(rs):
+        for r in rs:
+            u = RS_ORDER[r]
+            total = block_ref(r)[z].astype(F32)
+            if r < 13:
+                z_pair(r).wait_recv()
+                total += r3[r, 4].astype(F32)
+            else:
+                for j, copy in enumerate(z_direct(r)):
+                    copy.wait_recv()
+                    total += r3[r, j].astype(F32)
+            gsum[u] = total
+            square = total * total + EPS_ONE
+            m = [k for k in range(10) if u in UNIT_OF[k]][0]
+            row_o[...] += jnp.where(lane == m, jnp.sum(square, -1, keepdims=True), 0.0)
+            pack_o[u : u + 1, :] = jnp.sum(square, 0, keepdims=True)
+
+    def run(*events):
+        for stage, k in events:
+            stage(GROUPS[k])
+
+    load("dy", dy2_i, dy)
+    for r in range(4):
+        block_in(r).start()
+    for r in range(4, 8):
+        own_part(r).start()
+    load("o1", o1_i, o1)
+    load("w1", wa_i.at[pl.ds(4, 4)], wa.at[pl.ds(4, 4)])
+    load("qkv1", qkv1_i, qkv1)
+    load("h1", h1_i, h1)
+    load("y1", y1_i, y1)
+
+    def to_patch_half(src, dst, which):
+        own = pltpu.make_async_copy(src.at[:, mine], dst.at[pl.ds(t * fh, fh)], el.at[which])
+        own.start()
+        copy = remote(
+            src.at[:, theirs], dst.at[pl.ds(t * fh, fh)], es.at[which], er.at[which], other
+        )
+        copy.start()
+        return own, copy
+
+    def exchange_wait(started):
+        started[0].wait()
+        started[1].wait_recv()
+
+    lo_ex = to_patch_half(lo_i, lo_t, 0)
+    load("xt", xt_i, xt)
+    load("h0", h0_i, h0)
+    load("w0", wa_i.at[pl.ds(0, 4)], wa.at[pl.ds(0, 4)])
+    load("os", os_i, os_)
+    load("qkv0", qkv0_i, qkv0)
+
+    def tokens_out(src, dst, which, start, count):
+        span = pl.ds(start, count)
+        there = pl.ds(pl.multiple_of(t * half + start, 16), count)
+        own = pltpu.make_async_copy(
+            src.at[pl.ds(z * fr, fr), span], dst.at[z, :, there], tl.at[which]
+        )
+        own.start()
+        copies = []
+        for j, device in enumerate(along):
+            copy = remote(
+                src.at[pl.ds(device[1] * fr, fr), span],
+                dst.at[z, :, there],
+                ts.at[which, j],
+                tr.at[which, j],
+                device,
+            )
+            copy.start()
+            copies.append(copy)
+        return own, copies
+
+    def share(dst, several, which, start, count):
+        for started in several:
+            started[0].wait()
+            for copy in started[1]:
+                copy.wait_recv()
+        at = dst.at[:, :, pl.ds(pl.multiple_of(t * half + start, 16), count)]
+        copy = remote(at, at, ss.at[which], sr.at[which], other)
+        copy.start()
+        return copy
+
+    def transposed(src, dst):
+        lead = src.shape[0] // 2
+        for i in range(2):
+            dst[:, 384 * i : 384 * (i + 1)] = flat(src[lead * i : lead * (i + 1)]).T
+
+    def put_grad(dst, left, right):
+        def block(i, carry):
+            rows = pl.ds(pl.multiple_of(i * 384, 384), 384)
+            total = nn(left[rows, :], right()).astype(BF)
+            for h in range(2):
+                dst[h, i] = total[:, 384 * h : 384 * (h + 1)].reshape(wa.shape[3:])
+            return carry
+
+        lax.fori_loop(0, 2, block, 0)
+
+    def out_back(e_ref, u):
+        lead = e_ref.shape[0] // 2
+
+        def block(i, carry):
+            left = flat(e_ref[pl.ds(i * lead, lead)])
+            part = nn(left, wide(wa.at[u])).astype(BF)
+            do[pl.ds(i * fh, fh)] = part.reshape((fh,) + do.shape[1:])
+            return carry
+
+        lax.fori_loop(0, 2, block, 0)
+
+    zero = jnp.zeros((1, norm.shape[1]), F32)
+
+    def norm_branch(stack, block, u, values, run, gain, put, carry):
+        total = None
+        for s in range(3):
+            part = nt(flat(stack[(s,) + block]), wide(wa.at[u + s]))
+            total = part if total is None else total + part
+        dh[...] = total
+
+        def line(k, sums):
+            at = run(k)
+            up = dh[pl.ds(pl.multiple_of(k * LINES, LINES), LINES), :]
+            dv, dg = ln_back(flat(values[at]).astype(F32), gain, up)
+            put(at, dv)
+            return (
+                sums[0] + jnp.sum(dg, 0, keepdims=True),
+                sums[1] + jnp.sum(up, 0, keepdims=True),
+            )
+
+        return lax.fori_loop(0, dh.shape[0] // LINES, line, carry, unroll=2)
+
+    loads["dy"].wait()
+
+    def low_one(i, carry):
+        e[i] = dy[i].astype(BF)
+        return carry
+
+    lax.fori_loop(0, fh, low_one, 0)
+    run((send_one, 2), (send_in, 0), (send_in, 1), (send_one, 3))
+    loads["o1"].wait()
+    loads["w1"].wait()
+    out_back(e, 7)
+    transposed(e, et)
+    put_grad(wa.at[7], et, lambda: flat(o1[...]))
+    run((send_core, 4), (send_across, 0), (send_across, 1))
+    loads["qkv1"].wait()
+
+    def spatial(b, carry):
+        for s in range(3):
+            held[s] = qkv1[s, b]
+        held[3] = flat(do[pl.ds(2 * b, 2)])
+        for j in range(0, 6, 2):
+            group = head_lanes(j, 2)
+            parts = [[held[s, :, at] for at in group] for s in range(4)]
+            for s, outs in enumerate(attn_backward(*parts, None)):
+                for at, out in zip(group, outs):
+                    qkv1[s, b, :, at] = out
+
+        @pl.when(b == 0)
+        def _():
+            run((send_pair, 0), (send_pair, 1), (send_one, 4))
+
+        @pl.when(b == 1)
+        def _():
+            run((send_two, 2), (settle, 0), (settle, 1))
+
+        @pl.when(b == 2)
+        def _():
+            run((send_two, 3), (send_in, 2))
+
+        @pl.when(b == 3)
+        def _():
+            run((send_two, 4), (send_across, 2))
+
+        return carry
+
+    lax.fori_loop(0, fh, spatial, 0)
+    loads["h1"].wait()
+    loads["y1"].wait()
+
+    def put_two(at, dv):
+        total = dy[at] + dv
+        dy[at] = total
+        e[at] = total.astype(BF)
+
+    def spatial_block(i, carry):
+        return norm_branch(
+            qkv1,
+            (pl.ds(i * fh // 2, fh // 2),),
+            4,
+            y1,
+            lambda k: lines(y1, i * fh + k),
+            norm[1:2, :],
+            put_two,
+            carry,
+        )
+
+    dg1, db1 = lax.fori_loop(0, 2, spatial_block, (zero, zero))
+    e_ex = to_patch_half(e, e0, 1)
+    exchange_wait(lo_ex)
+    lo_out = [tokens_out(lo_t, lo_o, 0, 0, half)]
+    run((send_in, 3), (send_pair, 2))
+    transposed(h1, ht)
+    put_grad(wa.at[4], ht, lambda: flat(qkv1[0]))
+    put_grad(wa.at[5], ht, lambda: flat(qkv1[1]))
+    run((send_core, 5), (send_in, 4), (send_across, 3))
+    put_grad(wa.at[6], ht, lambda: flat(qkv1[2]))
+
+    transposed(e, et)
+    loads["w0"].wait()
+    loads["os"].wait()
+    exchange_wait(e_ex)
+    out_back(e0, 3)
+    put_grad(wa.at[3], et, lambda: flat(os_[...]))
+    run((send_core, 6), (send_one, 5), (send_across, 4), (send_pair, 3), (settle, 2))
+    loads["qkv0"].wait()
+    keep = same_patch(frames * 16, 2 * frames * 16, 16)
+
+    def temporal(b, carry):
+        rows = pl.ds(pl.multiple_of(b * 16, 16), 16)
+        n = frames * 16
+        for s in range(3):
+            held[s, 0:n] = flat(qkv0[s, :, rows])
+        held[3, 0:n] = flat(do[:, rows])
+        for j in range(0, 6, 3):
+            group = head_lanes(j, 3)
+            parts = [[held[s, 0:n, at] for at in group] for s in range(4)]
+            for s, outs in enumerate(attn_backward(*parts, keep)):
+                for at, out in zip(group, outs):
+                    qkv0[s, :, rows, at] = out.reshape((frames, 16, 128))
+        return carry
+
+    def put_one(at, dv):
+        total = flat(e0[at]).astype(F32) + dv
+        gt[at] = total.astype(BF).reshape((2, half // 2, dv.shape[1]))
+
+    def temporal_norm(i, sums):
+        span = slice(i * half // 2, (i + 1) * half // 2)
+        return norm_branch(
+            qkv0,
+            (slice(None), span),
+            0,
+            xt,
+            lambda k: (pl.ds(2 * k, 2), span),
+            norm[0:1, :],
+            put_one,
+            sums,
+        )
+
+    loads["xt"].wait()
+    lax.fori_loop(0, half // 32, temporal, 0)
+    run((send_one, 6), (send_two, 5), (send_pair, 4), (settle, 3))
+    sums = temporal_norm(0, (zero, zero))
+    gi_out = [tokens_out(gt, gi_o, 1, 0, half // 2)]
+    run((send_two, 6), (send_in, 5), (settle, 4))
+    loads["h0"].wait()
+    transposed(h0, ht)
+    lax.fori_loop(half // 32, half // 16, temporal, 0)
+    run((send_in, 6), (send_across, 5))
+    put_grad(tg.at[0], ht, lambda: flat(qkv0[0]))
+    put_grad(tg.at[1], ht, lambda: flat(qkv0[1]))
+    run((send_core, 7),)
+    put_grad(tg.at[2], ht, lambda: flat(qkv0[2]))
+    run((send_core, 8), (send_one, 7), (send_across, 6), (send_pair, 5))
+    sums = temporal_norm(1, sums)
+    gi_out.append(tokens_out(gt, gi_o, 2, half // 2, half // 2))
+    run((send_one, 8), (send_two, 7), (send_pair, 6), (settle, 5))
+    norm_rows = jnp.concatenate(
+        [sums[0], dg1, ng_i[2:3, :], sums[1], db1, ng_i[5:6, :], jnp.zeros((2, dg1.shape[1]), F32)],
+        0,
+    )
+    pack_o[16:24, :] = norm_rows[:, :384]
+    pack_o[24:32, :] = norm_rows[:, 384:]
+    run((send_two, 8), (send_in, 7), (settle, 6), (send_in, 8), (settle, 7))
+    run((settle, 8),)
+
+    first = remote(row_o, row_in, as_.at[0], ar.at[0], other)
+    first.start()
+    part = pl.ds(16, 16)
+    second = remote(pack_o.at[part], pack_in.at[0, part], as_.at[1], ar.at[1], other)
+    second.start()
+    lo_share = share(lo_o, lo_out, 0, 0, half)
+    gi_share = [share(gi_o, gi_out[:1], 1, 0, half // 2)]
+    first.wait()
+    second.wait()
+    row_o[...] = row_o[...] + row_in[...]
+    pack_o[16:32, :] = pack_o[16:32, :] + pack_in[0, 16:32, :]
+    pack_o[32:33, 0:128] = jnp.sum(row_o[...], 0, keepdims=True)
+    old = jnp.zeros((1, 128), F32)
+    mats = [(qkv_row[m // 3], m % 3) for m in range(6)]
+    mats += [(ref[...], k) for ref in (out_row, ffn_row) for k in range(2)]
+    for m, (values, k) in enumerate(mats):
+        old = jnp.where(lane[0:1] == m, jnp.sum(values[k : k + 1], -1, keepdims=True), old)
+    pack_o[32:33, 128:256] = old
+    for base, devices in ((1, (across_x, across_y, (3 - d, z, t))), (4, along)):
+        copies = []
+        for k, device in enumerate(devices):
+            copy = remote(
+                pack_o, pack_in.at[base + k], as_.at[1 + base + k], ar.at[1 + base + k], device
+            )
+            copy.start()
+            copies.append(copy)
+        if base == 4:
+            gi_share.append(share(gi_o, gi_out[1:], 2, half // 2, half // 2))
+        for copy in copies:
+            copy.wait()
+        pack_o[...] = (pack_o[...] + pack_in[base]) + (pack_in[base + 1] + pack_in[base + 2])
+
+    for r in range(16):
+        if r >= 8:
+            core_copy(r).wait_send()
+        if r >= 4:
+            one_copy(r).wait_send()
+            two_copy(r).wait_send()
+        for copy in [z_pair(r)] if r < 13 else z_direct(r):
+            copy.wait_send()
+
+    @pl.when(inner)
+    def _():
+        for r in range(13):
+            z_across(r).wait_send()
+
+    @pl.when(jnp.logical_not(inner))
+    def _():
+        for r in range(13):
+            z_in(r).wait_send()
+
+    for copy in (lo_ex[1], e_ex[1]):
+        copy.wait_send()
+    for started in lo_out + gi_out:
+        for copy in started[1]:
+            copy.wait_send()
+    for copy in [lo_share] + gi_share:
+        copy.wait_send()
+        copy.wait_recv()
+
+
+UNIT_OF = [(0,), (1,), (2,), (4,), (5,), (6,), (3,), (7,), (8, 10, 12, 14), (9, 11, 13, 15)]
+
+
+def update_kernel(
+    gsum,
+    row_sum,
+    pack,
+    qkv_row,
+    out_row,
+    ffn_row,
+    qkv_col,
+    out_col,
+    ffn_col,
+    qkvw,
+    outw,
+    ffnw,
+    norm,
+    moment,
+    lo,
+    gi,
+    lo_o,
+    gi_o,
+    norm_g,
+    norm_m,
+    norm_n,
+    qkv_g,
+    qkv_n,
+    out_g,
+    out_n,
+    ffn_g,
+    ffn_n,
+    qkv_r,
+    out_r,
+    ffn_r,
+    qkv_c,
+    out_c,
+    ffn_c,
+    rows_s,
+    cols_s,
+    mean_s,
+):
+    step = pl.program_id(0)
+    decay = 1.0 - STEP ** (-0.8)
+    width = norm.shape[1]
+    n = row_sum.shape[0]
+
+    @pl.when(step == 0)
+    def _():
+        lane = lax.broadcasted_iota(jnp.int32, (1, 128), 1)
+        across = jnp.where(lane < 8, 1.0 / width, 1.0 / (8 * 384))
+        old = jnp.concatenate(
+            [qkv_row[0], qkv_row[1], out_row[...], ffn_row[...], jnp.zeros((118, n), F32)], 0
+        )
+        row_new = decay * old.T + (1.0 - decay) * (row_sum[...] * across)
+        rows_s[...] = row_new
+        row_t = row_new.T
+        mean_s[...] = decay * (pack[32:33, 128:256] * (1.0 / width)) + (1.0 - decay) * (
+            pack[32:33, 0:128] * across * (1.0 / width)
+        )
+
+        def column(old_col, u):
+            fresh = decay * old_col + (1.0 - decay) * (pack[u : u + 1, :] * (1.0 / width))
+            cols_s[u : u + 1, :] = fresh
+            return fresh
+
+        for i in range(2):
+            qkv_r[i] = row_t[3 * i : 3 * i + 3]
+            for k in range(3):
+                qkv_c[i, k : k + 1, :] = column(qkv_col[i, k : k + 1, :], 4 * i + k)
+            out_c[i : i + 1, :] = column(out_col[i : i + 1, :], 4 * i + 3)
+            for c in range(4):
+                lanes = slice(384 * c, 384 * (c + 1))
+                ffn_c[i : i + 1, lanes] = column(ffn_col[i : i + 1, lanes], 8 + 2 * c + i)
+        out_r[...] = row_t[6:8]
+        ffn_r[...] = row_t[8:10]
+        grad = jnp.concatenate([pack[16:22, :], pack[24:30, :]], 1)
+        norm_g[...] = grad
+        fresh = decay * moment[...] + (1.0 - decay) * (grad * grad + EPS_ONE)
+        norm_m[...] = fresh
+        update = grad * lax.rsqrt(fresh)
+        rms = jnp.sqrt(jnp.mean(update * update, -1, keepdims=True))
+        norm_n[...] = norm[...] - RATE_NORM * (update / jnp.maximum(1.0, rms))
+
+    lo_o[...] = lo[...]
+    gi_o[...] = gi[...].astype(F32)
+
+    def change(k, m, u, rate):
+        second = (
+            rows_s[:, m : m + 1] * cols_s[u : u + 1, :] / mean_s[:, m : m + 1]
+        )
+        return rate * (gsum[k] * lax.rsqrt(second))
+
+    for i in range(2):
+
+        @pl.when(step == i)
+        def _():
+            for k in range(3):
+                qkv_g[0, k] = gsum[k]
+                qkv_n[0, k] = qkvw[0, k] - change(k, 3 * i + k, 4 * i + k, RATE_QKV)
+            out_g[0] = gsum[3]
+            out_n[0] = outw[0] - change(3, 6 + i, 4 * i + 3, RATE_OUT)
+
+        @pl.when(step == 2 + i)
+        def _():
+            for k in range(4):
+                c, m = k // 2, k % 2
+                lanes = slice(384 * c, 384 * (c + 1))
+                ffn_g[m, :, lanes] = gsum[k]
+                ffn_n[m, :, lanes] = ffnw[m, :, lanes] - change(
+                    k, 8 + m, 8 + 4 * i + k, (0.02, 0.01)[m]
+                )
+
+
+def call(kernel, outs, in_spaces, scratch, limit, collective=None, out_spaces=None):
+    extra = {}
+    if collective is not None:
+        extra = dict(collective_id=collective, has_side_effects=True)
+    out_spaces = out_spaces or [pltpu.VMEM] * len(outs)
+    return pl.pallas_call(
+        kernel,
+        out_shape=[jax.ShapeDtypeStruct(shape, kind) for shape, kind in outs],
+        in_specs=[pl.BlockSpec(memory_space=space) for space in in_spaces],
+        out_specs=[pl.BlockSpec(memory_space=space) for space in out_spaces],
+        scratch_shapes=scratch,
+        compiler_params=pltpu.CompilerParams(vmem_limit_bytes=limit, **extra),
+    )
+
+
+def per_device_kernels(
+    clips,
+    cotangent,
+    clip_counts,
+    norm_params,
+    norm_moment,
+    qkv_weight,
+    qkv_row,
+    qkv_col,
+    out_weight,
+    out_row,
+    out_col,
+    ffn_weight,
+    ffn_row,
+    ffn_col,
+):
+    slots, per, patches, width = clips.shape
+    frames = per * NZ
+    rows = qkv_weight.shape[2]
+    half = patches // 2
+    vm, hbm = pltpu.VMEM, pl.ANY
+    dma = pltpu.SemaphoreType.DMA
+    by_patch = (frames, half, width)
+    by_frame = (frames // 2, patches, width)
+    unit = (2, 2, NZ, rows, 384)
+    saved = [
+        ((8, 2) + unit, BF),
+        (by_patch, BF),
+        (by_patch, BF),
+        ((3,) + by_patch, BF),
+        (by_frame, BF),
+        (by_frame, F32),
+        (by_frame, BF),
+        ((3,) + by_frame, BF),
+        (by_frame, BF),
+        (by_frame, F32),
+        (by_frame, BF),
+        ((4,) + unit, BF),
+        ((4, NZ, rows, 384), BF),
+        ((8, width), F32),
+    ]
+    tokens = by_frame[0] * by_frame[1]
+    kept = call(
+        forward_kernel,
+        saved,
+        [hbm, hbm, vm, vm, vm, vm, pltpu.SMEM],
+        [
+            vm((8, 2) + unit, BF),
+            vm(by_patch, BF),
+            vm(by_frame, BF),
+            vm(by_patch, BF),
+            vm((3,) + by_patch, BF),
+            vm(by_patch, BF),
+            vm(by_frame, BF),
+            vm(by_frame, F32),
+            vm(by_frame, BF),
+            vm((3,) + by_frame, BF),
+            vm(by_frame, BF),
+            vm(by_frame, BF),
+            vm(by_patch, BF),
+            vm((frames, patches, width), BF),
+            vm((frames, patches, width), BF),
+            vm((width, 2 * tokens), BF),
+            vm((width, 2 * tokens), BF),
+            vm((frames, patches, width), F32),
+            vm((frames, patches, width), F32),
+            vm((2 * tokens, 768), BF),
+            vm((2 * tokens, 768), BF),
+            vm((8,) + unit, BF),
+            vm((4, 2, NZ, rows, 384), BF),
+            vm((4, NZ, rows, 384), BF),
+        ]
+        + [dma((16,))] * 11
+        + [
+            dma((2, 3)),
+            dma((2, 3)),
+            dma((2,)),
+            dma((3,)),
+            dma((3,)),
+            dma((4,)),
+            dma((40,)),
+        ]
+        + [dma((4,))] * 6,
+        LIMIT,
+        0,
+        [hbm] * 13 + [vm],
+    )(clips, cotangent, qkv_weight, out_weight, ffn_weight, norm_params, clip_counts)
+    clip_half = (slots, per, patches, width)
+    gsum, row_sum, pack, unused, layer_out, grad_low = call(
+        backward_kernel,
+        [
+            ((16, rows, 384), F32),
+            ((rows, 128), F32),
+            ((40, 384), F32),
+            (by_patch, BF),
+            (clip_half, BF),
+            (clip_half, BF),
+        ],
+        [hbm] * 13 + [vm] * 5,
+        [
+            vm((8, 2) + unit, BF),
+            vm(by_patch, BF),
+            vm(by_patch, BF),
+            vm((3,) + by_patch, BF),
+            vm(by_frame, BF),
+            vm(by_frame, F32),
+            vm(by_frame, BF),
+            vm((3,) + by_frame, BF),
+            vm(by_frame, BF),
+            vm(by_frame, F32),
+            vm(by_frame, BF),
+            vm((width, tokens), BF),
+            vm((width, tokens), BF),
+            vm(by_patch, BF),
+            vm(by_patch, BF),
+            vm(by_patch, BF),
+            vm((tokens // 2, width), F32),
+            vm((4,) + unit, BF),
+            vm((4, NZ, rows, 384), BF),
+            vm((3, 2) + unit, BF),
+            vm((8,) + unit, BF),
+            vm((12, 2, NZ, rows, 384), BF),
+            vm((12, NZ, rows, 384), BF),
+            vm((16, 5, rows, 384), BF),
+            dma((12,)),
+            dma((8,)),
+        ]
+        + [dma((16,))] * 12
+        + [
+            dma((2,)),
+            dma((2,)),
+            dma((2,)),
+            dma((3, 3)),
+            dma((3, 3)),
+            dma((3,)),
+            dma((3,)),
+            dma((3,)),
+            dma((8,)),
+            dma((8,)),
+            vm((rows, 128), F32),
+            vm((7, 40, 384), F32),
+            vm((4, patches, width), BF),
+        ],
+        LIMIT,
+        1,
+        [vm, vm, vm, hbm, hbm, hbm],
+    )(*kept[:13], norm_params, kept[13], qkv_row, out_row, ffn_row)
+    small = ((6, width), F32)
+    shapes = [(a.shape, F32) for a in (qkv_weight, out_weight, ffn_weight)]
+    states = (qkv_row, out_row, ffn_row, qkv_col, out_col, ffn_col)
+    whole = pl.BlockSpec(memory_space=vm)
+    clip = pl.BlockSpec((1,) + clip_half[1:], lambda c: (c, 0, 0, 0))
+    four = pl.BlockSpec((4, rows, 384), lambda c: (c, 0, 0))
+    one_qkv = pl.BlockSpec((1, 3, rows, 384), lambda c: (jnp.minimum(c, 1), 0, 0, 0))
+    one_out = pl.BlockSpec((1, rows, 384), lambda c: (jnp.minimum(c, 1), 0, 0))
+    half_ffn = pl.BlockSpec((2, rows, 768), lambda c: (0, 0, jnp.maximum(c - 2, 0)))
+    weights = [one_qkv, one_out, half_ffn]
+    outs = (
+        [(clip_half, BF), (clip_half, F32)]
+        + [small] * 3
+        + [shapes[0]] * 2
+        + [shapes[1]] * 2
+        + [shapes[2]] * 2
+        + [(a.shape, F32) for a in states]
+    )
+    results = pl.pallas_call(
+        update_kernel,
+        grid=(slots,),
+        out_shape=[jax.ShapeDtypeStruct(shape, kind) for shape, kind in outs],
+        in_specs=[four] + [whole] * 8 + weights + [whole] * 2 + [clip, clip],
+        out_specs=[clip, clip]
+        + [whole] * 3
+        + [spec for spec in weights for k in range(2)]
+        + [whole] * 6,
+        scratch_shapes=[vm((rows, 128), F32), vm((16, 384), F32), vm((1, 128), F32)],
+        compiler_params=pltpu.CompilerParams(vmem_limit_bytes=LIMIT),
+    )(
+        gsum,
+        row_sum,
+        pack,
+        *states,
+        qkv_weight,
+        out_weight,
+        ffn_weight,
+        norm_params,
+        norm_moment,
+        layer_out,
+        grad_low,
+    )
+    lo, gi, norm_g, norm_m, norm_n, *rest = results
+    qkv_g, qkv_n, out_g, out_n, ffn_g, ffn_n, *moments = rest
+    qkv_r, out_r, ffn_r, qkv_c, out_c, ffn_c = moments
+    return (
+        lo,
+        gi,
+        norm_g,
+        norm_m,
+        norm_n,
+        qkv_g,
+        qkv_n,
+        qkv_r,
+        qkv_c,
+        out_g,
+        out_n,
+        out_r,
+        out_c,
+        ffn_g,
+        ffn_n,
+        ffn_r,
+        ffn_c,
+    )
+
+
+LIMIT = 63 * 1024 * 1024
+
+
 def solution(mesh):
     in_specs = (
         P("dp", "seq", None, None),
@@ -394,6 +1955,8 @@
         P(None, ("dp", "seq")),
         P(None, "tensor"),
     )
+    sizes = dict(mesh.shape)
+    fits = sizes["dp"] == 4 and sizes["seq"] == NZ and sizes["tensor"] == 2
     return jax.shard_map(
-        per_device, mesh=mesh, in_specs=in_specs, out_specs=out_specs, check_vma=False
-    )
+        per_device_kernels if fits else per_device, mesh=mesh, in_specs=in_specs, out_specs=out_specs, check_vma=False
+    )

time: 1360 us -> 299 us (0.22)
  waiting for transfers between devices: 768 us -> 0 us
  Pallas kernels: 0 us -> 293 us
  matrix products: 178 us -> 0 us
  local copies, waits for them, and re-layouts: 154 us -> 3.77 us
  other arithmetic: 112 us -> 0 us
  blocking collectives: 80 us -> 0 us
  starting transfers between devices: 38.5 us -> 0 us
  between operations: 18 us -> 1.35 us
    pallas_call x0 -> x3, Pallas kernels: none -> 293 us  [the longest x1 146 us: per_device_kernels(): call(forward_kernel, saved, [hbm, hbm, vm, vm, vm, vm, pltpu.SMEM], [vm((...]
    unnamed x12 -> x0, waiting for transfers between devices: 230 us -> none
    dot_general x60 -> x0, matrix products: 178 us -> none  [the longest x4 17.3 us: attend_back(): jnp.einsum(form_pair(q_form, k_form, s_form), grad_heads, value_part, pre...]
    all_gather x3 -> x0, waiting for transfers between devices: 148 us -> none  [the longest x1 76.2 us: per_device(): lax.all_gather(shards[2], ('dp', 'seq'), axis=1, tiled=True)]
    psum x5 -> x0, waiting for transfers between devices: 142 us -> none  [tensor_total(): return lax.psum(partial_term, 'tensor')]
    all_to_all x8 -> x0, waiting for transfers between devices: 126 us -> none  [the longest x4 68 us: to_places(): lax.all_to_all(stacked, 'seq', split_axis=3, concat_axis=2, tiled=True)]
    reduce_scatter x2 -> x0, waiting for transfers between devices: 121 us -> none  [the longest x1 121 us: per_device(): lax.psum_scatter(weight_grads[2], ('dp', 'seq'), scatter_dimension=1, til...]
    psum x2 -> x0, blocking collectives: 80 us -> none  [the longest x1 77.5 us: per_device(): lax.psum((col_part[0], col_part[1], col_part[2], section_one[3], section_...]
  transfers between devices with their start and end apart: 19 -> 0, of which waited for: 15 -> 0; matrix products, arithmetic and copies ran while one was open for 17% -> 0% of each run, Pallas kernels for 0% -> 0%
where the time goes in v1:
time: 299 us; the launch traced here: 298 us
  Pallas kernels  293 us (98%)
  local copies, waits for them, and re-layouts  3.77 us (1%)
    pallas_call x1, Pallas kernels, per_device_kernels(): call(forward_kernel, saved, [hbm, hbm, vm, vm, vm, vm, pltpu.SMEM], [vm((...  146 us
    pallas_call x1, Pallas kernels, per_device_kernels(): call(backward_kernel, [((16, rows, 384), F32), ((rows, 128), F32), ((40,...  140 us
    pallas_call x1, Pallas kernels, per_device_kernels(): pl.pallas_call(update_kernel, grid=(slots,), out_shape=[jax.ShapeDtypeStr...  7.32 us

profile of v1, /device:TPU:0, one launch (start us, length us, event | category | flops | bytes accessed | tf_op | source)
XLA Modules:
  0.0 298.5 jit_solution(4338272815611280450)
XLA Ops:
  1.3 0.0 copy-start.1
  1.3 145.8 %shard_map.269 = (bf16[8,2,2,2,4,48,384]{6,5,4,3,2,1,0:T(8,128)(2,1)}, bf16[8,96,768]{2,1,0:T(8,128)(2,1)}, bf16[8,96,768]{2,1,0:T(8,128)(2,1)}, bf16[3,8,96,768...) custom-call(bf16[4,2,192,768]{3,2,1,0:T(8,128)(2,1)} %clips.1, ...), custom_call_target="tpu_custom_call" | custom-call | tf_op jit(solution)/shard_map/pallas_call | solution.py:1748
  147.1 0.0 copy-done.1
  147.1 0.6 copy.31.qkv_row
  147.7 0.0 copy-start
  147.7 140.2 %shard_map.270 = (f32[16,48,384]{2,1,0:T(8,128)}, f32[48,128]{1,0:T(8,128)}, f32[40,384]{1,0:T(8,128)}, bf16[8,96,768]{2,1,0:T(8,128)(2,1)}, bf16[4,2,192,768]{3...) custom-call(bf16[8,2,2,2,4,48,384]{6,5,4,3,2,1,0:T(8,128)(2,1)} %get-tuple-element.53.wa_i, ...), custom_call_target="tpu_custom_call" | custom-call | tf_op jit(solution)/shard_map/pallas_call | solution.py:1794
  288.0 0.0 copy-done
  288.0 0.6 copy.33.qkv_col
  288.6 7.3 %shard_map.271 = (bf16[4,2,192,768]{3,2,1,0:T(8,128)(2,1)}, f32[4,2,192,768]{3,2,1,0:T(8,128)}, f32[6,768]{1,0:T(8,128)}, f32[6,768]{1,0:T(8,128)}, f32[6,768]{1...) custom-call(f32[16,48,384]{2,1,0:T(8,128)} %get-tuple-element.67.gsu, ...), custom_call_target="tpu_custom_call" | custom-call | tf_op jit(solution)/shard_map/pallas_call | solution.py:1871
  295.9 1.3 copy.35
  297.2 1.3 copy.34
Async XLA Ops:
  1.3 145.8 %copy-start.1 = (f32[2,3,48]{2,0,1:T(2,128)S(1)}, f32[2,3,48]{2,0,1:T(2,128)}, u32[]{:S(2)}) copy-start(f32[2,3,48]{2,0,1:T(2,128)} %param.20) | copy-start | bytes 3460
  147.7 140.3 %copy-start = (f32[2,3,384]{2,0,1:T(2,128)S(1)}, f32[2,3,384]{2,0,1:T(2,128)}, u32[]{:S(2)}) copy-start(f32[2,3,384]{2,0,1:T(2,128)} %param.21) | copy-start | bytes 27652
